TPU v7x, 128 devices: a whole 4x4x4 slice. The times are simulated.
128 devices in a mesh: stream: 4 (over y), azim: 8 (over x_lo, z), normal: 4 (over x_hi, core).
Axes of the slice: x: 4 (x_hi: 2, x_lo: 2; x = x_hi * 2 + x_lo), y: 4, z: 4, core: 2. Of those that a mesh axis runs over, the one named last changes fastest.
Arguments:
- perturbation: float32 [12, 32, 384, 1024], P(None, 'stream', 'normal', 'azim'), may hold values from -6 to 6
- base_flow: bfloat16 [8, 32, 384, 1024], P(None, 'stream', 'normal', 'azim'), may hold values from 0.25 to 2
- stream_ops: bfloat16 [2, 32, 32], replicated, may hold values from -1 to 1
- azimuth_ops: bfloat16 [2, 1024, 1024], replicated, may hold values from -0.1875 to 0.1875
- normal_ops: bfloat16 [2, 384, 384], replicated, may hold values from -0.3125 to 0.3125
- coupling: float32 [3, 12, 12], replicated, may hold values from -1.75 to 1.75
- chemistry: float32 [3, 12, 12], replicated, may hold values from -1.75 to 1.75
Outputs:
- advanced: float32 [12, 32, 384, 1024], P(None, 'stream', 'normal', 'azim')
All inputs are finite; a program needn't handle non-finite values.
Results may differ from a plain program's by a relative error of at most 0.0019.
Values may be sent and summed in bfloat16 or wider, within the bound.
A program may use at most 256 MiB of HBM per device.

v0:
```python
import jax
import jax.numpy as jnp
from jax import lax
from jax.sharding import PartitionSpec as P

highest = lax.Precision.HIGHEST


def along_last(lines, operators):
    dims = (((lines.ndim - 1,), (1,)), ((), ()))
    first_der = lax.dot_general(lines, operators[0], dims, preferred_element_type=jnp.float32)
    second_der = lax.dot_general(lines, operators[1], dims, preferred_element_type=jnp.float32)
    return (first_der, second_der)


def flux_terms(first_der, second_der, velocity, density, viscous, coupling_d):
    mixed = jnp.einsum("vw,wxyz->vxyz", coupling_d, first_der, precision=highest)
    return (
        -velocity.astype(jnp.float32) * first_der
        - density.astype(jnp.float32) * mixed
        + viscous.astype(jnp.float32) * second_der
    )


def shards(perturbation, base_flow, stream_ops, azimuth_ops, normal_ops, coupling, chemistry):
    lowered = perturbation.astype(jnp.bfloat16)
    normal_base = jnp.stack([base_flow[2], base_flow[3], base_flow[4]])
    lines_q = lax.all_to_all(lowered, "normal", split_axis=3, concat_axis=2, tiled=True)
    lines_base = lax.all_to_all(normal_base, "normal", split_axis=3, concat_axis=2, tiled=True)
    turned = jnp.swapaxes(lines_q, 2, 3)
    turned_base = jnp.swapaxes(lines_base, 2, 3)
    first_der, second_der = along_last(turned, normal_ops)
    normal_terms = flux_terms(
        first_der, second_der, turned_base[0], turned_base[1], turned_base[2], coupling[2]
    )
    normal_flux = lax.all_to_all(
        jnp.swapaxes(normal_terms, 2, 3), "normal", split_axis=2, concat_axis=3, tiled=True
    )
    azim_base = jnp.stack([base_flow[1], base_flow[3], base_flow[4]])
    lines_q = lax.all_to_all(lowered, "azim", split_axis=2, concat_axis=3, tiled=True)
    lines_base = lax.all_to_all(azim_base, "azim", split_axis=2, concat_axis=3, tiled=True)
    first_der, second_der = along_last(lines_q, azimuth_ops)
    azim_terms = flux_terms(
        first_der, second_der, lines_base[0], lines_base[1], lines_base[2], coupling[1]
    )
    azim_flux = lax.all_to_all(azim_terms, "azim", split_axis=3, concat_axis=2, tiled=True)
    stream_base = jnp.stack([base_flow[0], base_flow[3], base_flow[4]])
    lines_q = lax.all_to_all(lowered, "stream", split_axis=2, concat_axis=1, tiled=True)
    lines_base = lax.all_to_all(stream_base, "stream", split_axis=2, concat_axis=1, tiled=True)
    turned = jnp.moveaxis(lines_q, 1, 3)
    turned_base = jnp.moveaxis(lines_base, 1, 3)
    first_der, second_der = along_last(turned, stream_ops)
    stream_terms = flux_terms(
        first_der, second_der, turned_base[0], turned_base[1], turned_base[2], coupling[0]
    )
    stream_flux = lax.all_to_all(
        jnp.moveaxis(stream_terms, 3, 1), "stream", split_axis=1, concat_axis=2, tiled=True
    )
    parts = jnp.einsum("cvw,wsna->cvsna", chemistry, perturbation, precision=highest)
    source = (
        parts[0]
        + base_flow[5].astype(jnp.float32) * parts[1]
        + base_flow[6].astype(jnp.float32) * parts[2]
        - base_flow[7].astype(jnp.float32) * perturbation
    )
    rate = normal_flux + azim_flux + stream_flux + source
    variable_ids = jnp.arange(perturbation.shape[0], dtype=jnp.int32)
    wall_start = lax.axis_index("normal") * perturbation.shape[2]
    wall_rows = jnp.arange(perturbation.shape[2], dtype=jnp.int32) + wall_start == 0
    held = (variable_ids >= 5) & (variable_ids <= 9)
    pinned = held[:, None, None, None] & wall_rows[None, None, :, None]
    rate = jnp.where(pinned, jnp.float32(0.0), rate)
    return perturbation + 0.2 * rate


def solution(mesh):
    return jax.shard_map(
        shards,
        mesh=mesh,
        in_specs=(
            P(None, "stream", "normal", "azim"),
            P(None, "stream", "normal", "azim"),
            P(),
            P(),
            P(),
            P(),
            P(),
        ),
        out_specs=P(None, "stream", "normal", "azim"),
        check_vma=False,
    )
```

profile of v0, /device:TPU:1, one launch (start us, length us, event | category | flops | bytes accessed | tf_op | source)
XLA Modules:
  0.0 636.8 jit_solution(11661185604476431672)
XLA Ops:
  0.0 2.4 bitcast_convert_fusion.2
  2.4 1.0 slice.103
  3.4 0.1 copy.252
  3.6 0.2 copy.253
  3.8 1.1 pad_maximum_fusion.1
  4.9 5.0 all-to-all-start.6
  9.9 0.4 copy.251
  10.3 8.8 %all-to-all-done.6 = bf16[3,8,96,128]{3,1,0,2:T(8,128)(2,1)S(1)} async-done(((bf16[3,8,96,128]{3,1,0,2:T(8,128)(2,1)}), bf16[3,8,96,128]{3,1,0,2:T(8,128)(2,1)S(1)}, u32[]{:S(2)}, u32[]{:S(2)}) %all-to-all-start.6) | async-done | bytes 589856 | tf_op jit(solution)/shard_map/all_to_all | solution.py:49
  19.2 18.2 %all_to_all.159 = bf16[3,8,96,128]{2,1,0,3:T(8,128)(2,1)} all-to-all(bf16[3,8,96,128]{2,1,0,3:T(8,128)(2,1)S(1)} %copy.251), channel_id=1, replica_groups=mesh['stream'=4,'azim'=8,'normal'=4] {'normal'}, dimensions={3} | all-to-all | bytes 1179648 | tf_op jit(solution)/shard_map/all_to_all | solution.py:29
  37.3 5.1 all-to-all-start.3
  42.4 2.8 convert_element_type.54
  45.2 2.3 copy.198
  47.6 2.9 all-to-all-done.3
  50.4 4.5 all-to-all-start.7
  54.9 3.0 copy.186
  57.9 23.0 %all-to-all-done.7 = bf16[12,8,96,128]{3,1,0,2:T(8,128)(2,1)} async-done(((bf16[12,8,96,128]{3,1,0,2:T(8,128)(2,1)}), bf16[12,8,96,128]{3,1,0,2:T(8,128)(2,1)}, u32[]{:S(2)}, u32[]{:S(2)}) %all-to-all-start.7) | async-done | bytes 2359328 | tf_op jit(solution)/shard_map/all_to_all | solution.py:48
  80.9 7.8 %all-to-all-start.1 = ((bf16[12,8,96,128]{2,1,0,3:T(8,128)(2,1)}), bf16[12,8,96,128]{2,1,0,3:T(8,128)(2,1)S(1)}, u32[]{:S(2)}, u32[]{:S(2)}) async-start(bf16[12,8,96,128]{2,1,0,3:T(8,128)(2,1)} %copy.186), calls=%async_computation.1 | async-start | bytes 6291456 | tf_op jit(solution)/shard_map/all_to_all | solution.py:28
  88.8 2.0 copy.310
  90.8 35.6 %all-to-all-done.1 = bf16[12,8,96,128]{2,1,0,3:T(8,128)(2,1)S(1)} async-done(((bf16[12,8,96,128]{2,1,0,3:T(8,128)(2,1)}), bf16[12,8,96,128]{2,1,0,3:T(8,128)(2,1)S(1)}, u32[]{:S(2)}, u32[]{:S(2)}) %all-to-all-start.1) | async-done | bytes 2359328 | tf_op jit(solution)/shard_map/all_to_all | solution.py:28
  126.3 5.8 all-to-all-start.4
  132.1 1.0 negate_bitcast_fusion
  133.1 1.1 convert_bitcast_fusion.1
  134.2 2.4 fusion.23
  136.7 9.2 %fusion.4 = f32[24,128,32,12]{1,3,2,0:T(8,128)S(1)} fusion(f32[12,24,128,32]{2,3,1,0:T(8,128)S(1)} %fusion.23, f32[3,12,12]{2,1,0:T(8,128)S(1)} %copy-done.14), kind=kOutput, calls=%fused_computation.5 | convolution fusion | flops 169869312 | bytes 9445376 | tf_op jit(solution)/shard_map/vw,wxyz->vxyz/dot_general | solution.py:17
  145.9 6.1 fusion.19
  152.0 4.9 copy.221
  156.9 4.1 all-to-all-done.4
  161.0 4.9 all-to-all-start.8
  165.9 2.6 copy.185
  168.6 2.4 all_to_all.118
  171.0 1.7 negate_bitcast_fusion.1
  172.8 2.0 convert_bitcast_fusion.3
  174.7 4.1 copy.188
  178.8 5.2 all_to_all.122
  184.0 1.6 fusion.29
  185.7 9.8 %fusion.8 = f32[8,32,384,12]{2,3,1,0:T(8,128)S(1)} fusion(f32[12,8,32,384]{3,2,1,0:T(8,128)S(1)} %fusion.29, f32[3,12,12]{2,1,0:T(8,128)S(1)} %copy-done.14), kind=kOutput, calls=%fused_computation.10 | convolution fusion | flops 169869312 | bytes 9445376 | tf_op jit(solution)/shard_map/vw,wxyz->vxyz/dot_general | solution.py:17
  195.5 6.1 fusion.21
  201.7 16.0 %copy.191 = f32[12,8,384,32]{3,1,0,2:T(8,128)} copy(f32[12,8,384,32]{2,3,1,0:T(8,128)} %fusion.21) | data formatting | bytes 9437184 | tf_op jit(solution)/shard_map/add | solution.py:19
  217.7 21.8 %reshape.97 = f32[4,1,294912]{2,1,0:T(1,128)} reshape(f32[384,12,8,32]{3,2,1,0:T(8,128)} %bitcast.252) | data formatting | bytes 9437184
  239.4 5.9 all-to-all-start.2
  245.4 0.1 copy.195
  245.6 0.2 copy.241
  245.9 0.2 copy.242
  246.2 0.2 copy.239
  246.5 4.6 copy.247
  251.1 5.8 reshape.96
  256.9 6.1 fusion.36
  263.0 12.0 %fusion.6 = f32[8,12,1024,12]{2,3,1,0:T(8,128)S(1)} fusion(f32[12,8,12,1024]{3,2,1,0:T(8,128)S(1)} %fusion.36, f32[3,12,12]{2,1,0:T(8,128)S(1)} %copy-done.14), kind=kOutput, calls=%fused_computation.8 | convolution fusion | flops 169869312 | bytes 11018240 | tf_op jit(solution)/shard_map/vw,wxyz->vxyz/dot_general | solution.py:17
  275.1 10.2 %fusion.2 = f32[12,8,12,1024]{3,2,1,0:T(8,128)} fusion(f32[8,12,1024,12]{2,3,1,0:T(8,128)S(1)} %fusion.6, f32[12,8,12,1024]{3,2,1,0:T(8,128)S(1)} %fusion.36, f32[8,12,1024]{2,1,0:T(8,128)S(1)} %reshape.95, f32[8,12,1024]{2,1,0:T(8,128)S(1)} %reshape.94, f32[8,12,1024]{2,1,0:T(8,128)S(1)} %reshape.93, bf16[12,8,12,1024]{3,2,1,0:T(8,128)(2,1)S(1)} %copy-done.2, ...), kind=kOutput, calls=%fused_computation.3 | convolution fusion | flops 2421817344 | bytes 24117248 | tf_op jit(solution)/shard_map/dot_general | solution.py:12
  285.3 39.5 %copy.209 = f32[12,8,12,1024]{2,1,0,3:T(8,128)} copy(f32[12,8,12,1024]{3,2,1,0:T(8,128)} %fusion.2) | data formatting | bytes 9437184 | tf_op jit(solution)/shard_map/add | solution.py:19
  324.8 82.2 %reshape.99 = f32[8,1,147456]{2,1,0:T(1,128)} reshape(f32[1024,12,8,12]{3,2,1,0:T(8,128)} %bitcast.250) | data formatting | bytes 9437184
  406.9 4.9 all-to-all-start.5
  411.9 18.6 %fusion = f32[3,12,8,96,128]{4,1,3,2,0:T(8,128)S(1)} fusion(f32[12,8,96,128]{3,2,1,0:T(8,128)} %param.7, f32[3,12,12]{2,1,0:T(8,128)S(1)} %copy-done), kind=kOutput, calls=%fused_computation | convolution fusion | flops 509607936 | bytes 18876096 | tf_op jit(solution)/shard_map/cvw,wsna->cvsna/dot_general | solution.py:59
  430.5 6.6 %fusion.57 = (f32[1,12,8,96,128]{4,1,3,2,0:T(8,128)}, f32[1,12,8,96,128]{4,1,3,2,0:T(8,128)}, f32[1,12,8,96,128]{4,1,3,2,0:T(8,128)}) fusion(f32[3,12,8,96,128]{4,1,3,2,0:T(8,128)S(1)} %fusion), kind=kLoop, calls=%fused_computation.88 | loop fusion | bytes 28311552 | tf_op jit(solution)/shard_map/slice | solution.py:61
  437.1 5.1 copy.222
  442.2 0.5 broadcast.55
  442.7 17.5 %reduce = f32[4,294912]{1,0:T(4,128)} reduce(f32[4,1,294912]{2,1,0:T(1,128)} %all-to-all-done.2, f32[]{:T(128)} %broadcast.55), dimensions={1}, to_apply=%all_to_all.123.reduce_sub_computation | reduce | bytes 9437188 | tf_op jit(solution)/shard_map/all_to_all | solution.py:36
  460.3 15.3 %reshape.98 = f32[384,12,8,32]{3,2,1,0:T(8,128)} reshape(f32[4,294912]{1,0:T(4,128)} %reduce) | data formatting | bytes 9437184
  475.5 12.9 %copy.192 = f32[12,8,4,96,32]{3,4,2,1,0:T(8,128)} copy(f32[12,8,4,96,32]{4,1,0,3,2:T(8,128)} %bitcast.253) | data formatting | bytes 9437184 | tf_op jit(solution)/shard_map/all_to_all | solution.py:36
  488.5 6.1 copy.212
  494.6 16.1 %reduce.1 = f32[8,147456]{1,0:T(8,128)} reduce(f32[8,1,147456]{2,1,0:T(1,128)} %all-to-all-done.5, f32[]{:T(128)} %broadcast.55), dimensions={1}, to_apply=%all_to_all.134.reduce_sub_computation | reduce | bytes 9437188 | tf_op jit(solution)/shard_map/all_to_all | solution.py:46
  510.7 76.9 %reshape.100 = f32[1024,12,8,12]{3,2,1,0:T(8,128)} reshape(f32[8,147456]{1,0:T(8,128)} %reduce.1) | data formatting | bytes 9437184
  587.6 30.6 %copy.211 = f32[12,8,8,12,128]{4,1,3,2,0:T(8,128)} copy(f32[12,8,8,12,128]{3,1,0,4,2:T(8,128)} %bitcast.251) | data formatting | bytes 9437184 | tf_op jit(solution)/shard_map/all_to_all | solution.py:46
  618.2 18.1 %fusion.16 = f32[12,8,96,128]{3,2,1,0:T(8,128)} fusion(f32[12,8,96,128]{3,2,1,0:T(8,128)} %param.7, f32[1,12,8,96,128]{4,1,3,2,0:T(8,128)} %get-tuple-element.7, f32[1,12,8,96,128]{4,1,3,2,0:T(8,128)} %get-tuple-element.6, f32[1,12,8,96,128]{4,1,3,2,0:T(8,128)} %get-tuple-element.5, f32[12,4,8,24,128]{4,3,1,2,0:T(8,128)} %copy.222, ...), kind=kLoop, calls=%fused_computation.19 | loop fusion | flops 14155776 | bytes 38929536 | tf_op jit(solution)/shard_map/add | solution.py:73
  (46 shorter events, 0.5 us)
Async XLA Ops:
  0.0 411.9 %copy-start = (f32[3,12,12]{2,1,0:T(8,128)S(1)}, f32[3,12,12]{2,1,0:T(8,128)}, u32[]{:S(2)}) copy-start(f32[3,12,12]{2,1,0:T(8,128)} %param.13) | copy-start | bytes 5188
  0.0 9.9 %slice-start = ((bf16[8,8,96,128]{3,2,1,0:T(8,128)(2,1)}), bf16[3,8,96,128]{3,2,1,0:T(8,128)(2,1)S(1)}, s32[]{:S(2)}) async-start(bf16[8,8,96,128]{3,2,1,0:T(8,128)(2,1)} %param.8), calls=%async_computation.9 | async-start | bytes 1179648 | tf_op jit(solution)/shard_map/slice | solution.py:27
  4.9 14.3 %all-to-all-start.6 = ((bf16[3,8,96,128]{3,1,0,2:T(8,128)(2,1)}), bf16[3,8,96,128]{3,1,0,2:T(8,128)(2,1)S(1)}, u32[]{:S(2)}, u32[]{:S(2)}) async-start(bf16[3,8,96,128]{3,1,0,2:T(8,128)(2,1)} %get-tuple-element.20), calls=%async_computation.6 | async-start | bytes 1179648 | tf_op jit(solution)/shard_map/all_to_all | solution.py:49
  19.2 18.2 %copy-start.5 = (bf16[3,8,96,128]{3,1,0,2:T(8,128)(2,1)}, bf16[3,8,96,128]{3,1,0,2:T(8,128)(2,1)S(1)}, u32[]{:S(2)}) copy-start(bf16[3,8,96,128]{3,1,0,2:T(8,128)(2,1)S(1)} %all-to-all-done.6) | copy-start | bytes 1769476
  37.3 13.1 %all-to-all-start.3 = ((bf16[3,8,96,128]{3,1,0,2:T(8,128)(2,1)}), bf16[3,8,96,128]{3,1,0,2:T(8,128)(2,1)S(1)}, u32[]{:S(2)}, u32[]{:S(2)}) async-start(bf16[3,8,96,128]{3,1,0,2:T(8,128)(2,1)} %get-tuple-element.19), calls=%async_computation.3 | async-start | bytes 1179648 | tf_op jit(solution)/shard_map/all_to_all | solution.py:41
  50.4 7.5 %copy-start.3 = (bf16[3,8,96,128]{3,1,0,2:T(8,128)(2,1)}, bf16[3,8,96,128]{3,1,0,2:T(8,128)(2,1)S(1)}, u32[]{:S(2)}) copy-start(bf16[3,8,96,128]{3,1,0,2:T(8,128)(2,1)S(1)} %all-to-all-done.3) | copy-start | bytes 1769476
  50.4 30.5 %all-to-all-start.7 = ((bf16[12,8,96,128]{3,1,0,2:T(8,128)(2,1)}), bf16[12,8,96,128]{3,1,0,2:T(8,128)(2,1)}, u32[]{:S(2)}, u32[]{:S(2)}) async-start(bf16[12,8,96,128]{3,1,0,2:T(8,128)(2,1)} %copy.198), calls=%async_computation.7 | async-start | bytes 4718592 | tf_op jit(solution)/shard_map/all_to_all | solution.py:48
  80.9 45.4 %all-to-all-start.1 = ((bf16[12,8,96,128]{2,1,0,3:T(8,128)(2,1)}), bf16[12,8,96,128]{2,1,0,3:T(8,128)(2,1)S(1)}, u32[]{:S(2)}, u32[]{:S(2)}) async-start(bf16[12,8,96,128]{2,1,0,3:T(8,128)(2,1)} %copy.186), calls=%async_computation.1 | async-start | bytes 6291456 | tf_op jit(solution)/shard_map/all_to_all | solution.py:28
  88.8 45.5 %copy-start.15 = (bf16[2,32,32]{2,1,0:T(8,128)(2,1)S(1)}, bf16[2,32,32]{2,1,0:T(8,128)(2,1)}, u32[]{:S(2)}) copy-start(bf16[2,32,32]{2,1,0:T(8,128)(2,1)} %param.9) | copy-start | bytes 12292
  126.3 34.6 %all-to-all-start.4 = ((bf16[12,8,96,128]{3,1,0,2:T(8,128)(2,1)}), bf16[12,8,96,128]{3,1,0,2:T(8,128)(2,1)}, u32[]{:S(2)}, u32[]{:S(2)}) async-start(bf16[12,8,96,128]{3,1,0,2:T(8,128)(2,1)} %copy.198), calls=%async_computation.4 | async-start | bytes 4718592 | tf_op jit(solution)/shard_map/all_to_all | solution.py:40
  132.1 4.5 copy-start.14
  161.0 78.5 %all-to-all-start.8 = ((f32[12,32,24,128]{3,2,0,1:T(8,128)}), f32[12,32,24,128]{3,2,0,1:T(8,128)}, u32[]{:S(2)}, u32[]{:S(2)}) async-start(f32[12,32,24,128]{3,2,0,1:T(8,128)} %copy.221), calls=%async_computation.8 | async-start | bytes 9437184 | tf_op jit(solution)/shard_map/all_to_all | solution.py:56
  178.8 5.2 copy-start.13
  185.6 9.9 %copy-start.9 = (f32[8,384,32]{1,2,0:T(8,128)S(1)}, f32[8,384,32]{1,2,0:T(8,128)}, u32[]{:S(2)}) copy-start(f32[8,384,32]{1,2,0:T(8,128)} %negate_bitcast_fusion.1) | copy-start | bytes 1179652
  185.6 9.9 %copy-start.10 = (f32[8,384,32]{1,2,0:T(8,128)S(1)}, f32[8,384,32]{1,2,0:T(8,128)}, u32[]{:S(2)}) copy-start(f32[8,384,32]{1,2,0:T(8,128)} %get-tuple-element.15) | copy-start | bytes 1179652
  185.7 9.9 %copy-start.11 = (f32[8,384,32]{1,2,0:T(8,128)S(1)}, f32[8,384,32]{1,2,0:T(8,128)}, u32[]{:S(2)}) copy-start(f32[8,384,32]{1,2,0:T(8,128)} %get-tuple-element.16) | copy-start | bytes 1179652
  239.4 5.9 copy-start.4
  239.4 167.5 %all-to-all-start.2 = ((f32[4,1,294912]{2,1,0:T(1,128)}), f32[4,1,294912]{2,1,0:T(1,128)}, u32[]{:S(2)}, u32[]{:S(2)}) async-start(f32[4,1,294912]{2,1,0:T(1,128)} %reshape.97), calls=%async_computation.2 | async-start | bytes 9437184 | tf_op jit(solution)/shard_map/all_to_all | solution.py:36
  263.0 12.1 %copy-start.2 = (bf16[12,8,12,1024]{3,2,1,0:T(8,128)(2,1)S(1)}, bf16[12,8,12,1024]{3,2,1,0:T(8,128)(2,1)}, u32[]{:S(2)}) copy-start(bf16[12,8,12,1024]{3,2,1,0:T(8,128)(2,1)} %reshape.96) | copy-start | bytes 7077892
  263.0 12.1 %copy-start.12 = (bf16[2,1024,1024]{2,1,0:T(8,128)(2,1)S(1)}, bf16[2,1024,1024]{2,1,0:T(8,128)(2,1)}, u32[]{:S(2)}) copy-start(bf16[2,1024,1024]{2,1,0:T(8,128)(2,1)} %param.10) | copy-start | bytes 12582916
  406.9 87.7 %all-to-all-start.5 = ((f32[8,1,147456]{2,1,0:T(1,128)}), f32[8,1,147456]{2,1,0:T(1,128)}, u32[]{:S(2)}, u32[]{:S(2)}) async-start(f32[8,1,147456]{2,1,0:T(1,128)} %reshape.99), calls=%async_computation.5 | async-start | bytes 9437184 | tf_op jit(solution)/shard_map/all_to_all | solution.py:46
  587.6 30.7 %copy-start.6 = (f32[8,96,128]{2,1,0:T(8,128)S(1)}, f32[8,96,128]{2,1,0:T(8,128)}, u32[]{:S(2)}) copy-start(f32[8,96,128]{2,1,0:T(8,128)} %get-tuple-element.8) | copy-start | bytes 1179652
  587.6 30.7 %copy-start.7 = (f32[8,96,128]{2,1,0:T(8,128)S(1)}, f32[8,96,128]{2,1,0:T(8,128)}, u32[]{:S(2)}) copy-start(f32[8,96,128]{2,1,0:T(8,128)} %get-tuple-element.11) | copy-start | bytes 1179652
  587.6 30.7 %copy-start.8 = (f32[8,96,128]{2,1,0:T(8,128)S(1)}, f32[8,96,128]{2,1,0:T(8,128)}, u32[]{:S(2)}) copy-start(f32[8,96,128]{2,1,0:T(8,128)} %get-tuple-element.12) | copy-start | bytes 1179652
  618.2 18.2 %copy-start.1 = (f32[3,12,12]{2,1,0:T(8,128)S(1)}, f32[3,12,12]{2,1,0:T(8,128)}, u32[]{:S(2)}) copy-start(f32[3,12,12]{2,1,0:T(8,128)} %param.13) | copy-start | bytes 5188
where the time goes:
time: 643 us; the launch traced here: 637 us
  local copies, waits for them, and re-layouts  353 us (55%)
  matrix products  82.2 us (13%)
  waiting for transfers between devices  74.3 us (12%)
  other arithmetic  64.1 us (10%)
  starting transfers between devices  43.9 us (7%)
  blocking collectives  18.2 us (3%)
    unnamed x40, local copies, waits for them, and re-layouts  197 us
    add x3, local copies, waits for them, and re-layouts, flux_terms(): -velocity.astype(jnp.float32) * first_der  60.4 us
    all_to_all x1, waiting for transfers between devices, shards(): lax.all_to_all(lowered, 'normal', split_axis=3, concat_axis=2, tiled=True)  35.6 us
    dot_general x3, matrix products, flux_terms(): jnp.einsum('vw,wxyz->vxyz', coupling_d, first_der, precision=highest)  31.1 us
    all_to_all x1, local copies, waits for them, and re-layouts, shards(): lax.all_to_all(azim_terms, 'azim', split_axis=3, concat_axis=2, tiled=True)  30.6 us
    all_to_all x1, waiting for transfers between devices, shards(): lax.all_to_all(lowered, 'stream', split_axis=2, concat_axis=1, tiled=True)  23 us
    dot_general x3, matrix products, along_last(): lax.dot_general(lines, operators[1], dims, preferred_element_type=jnp.flo...  22.4 us
    all_to_all x3, local copies, waits for them, and re-layouts, shards(): lax.all_to_all(jnp.swapaxes(normal_terms, 2, 3), 'normal', split_axis=2,...  19.5 us
  transfers between devices with their start and end apart: 8, of which 5 were waited for; matrix products, arithmetic and copies ran while one was open for 54% of the time, Pallas kernels for 0%

commit v1 on v0

v1 whole, which is shorter than its diff:
```python
import functools

import jax
import jax.numpy as jnp
from jax import lax
from jax.experimental import pallas as pl
from jax.experimental.pallas import tpu as pltpu
from jax.sharding import PartitionSpec as P

MESH = pl.DeviceIdType.MESH
F32, BF16 = jnp.float32, jnp.bfloat16
NV, S, N, A = 12, 8, 96, 128


def copies_table():
    table, count = {}, 0
    for t in range(2):
        for d in (1, 2, 3):
            for name in ("zf", "zb", "zr"):
                table[name, t, d] = count
                count += 1
        for d in range(4):
            for name in ("lo", "hi", "co", "cw"):
                table[name, t, d] = count
                count += 1
    for g in range(3):
        for d in (1, 2, 3):
            for name in ("yf", "yr"):
                table[name, g, d] = count
                count += 1
    return table, count


TABLE, COPIES = copies_table()


def spread(matrix, reps):
    rows, cols = matrix.shape
    shift = reps.bit_length() - 1
    up = (lax.broadcasted_iota(jnp.int32, (rows * reps, rows), 0) >> shift
          == lax.broadcasted_iota(jnp.int32, (rows * reps, rows), 1)).astype(F32).astype(BF16)
    wide = (lax.broadcasted_iota(jnp.int32, (cols, cols * reps), 1) >> shift
            == lax.broadcasted_iota(jnp.int32, (cols, cols * reps), 0)).astype(F32).astype(BF16)
    tall = jnp.dot(up, matrix, preferred_element_type=F32).astype(BF16)
    full = jnp.dot(tall, wide, preferred_element_type=F32)
    r = lax.broadcasted_iota(jnp.int32, full.shape, 0) & (reps - 1)
    c = lax.broadcasted_iota(jnp.int32, full.shape, 1) & (reps - 1)
    return jnp.where(r == c, full, 0.0).astype(BF16)


def split_two(matrix):
    high = matrix.astype(BF16)
    return high, (matrix - high.astype(F32)).astype(BF16)


def kernel(pert, base, sops, aops, nops, coup, chem, out,
           zs, zbs, gat, zbase, oth, ys, yr, fy, ry, fz, rz, dn, dy, wa, kc, ky, kz, ks, kn,
           ssem, rsem, lsem):
    y = lax.axis_index("stream")
    ai = lax.axis_index("azim")
    ni = lax.axis_index("normal")
    lo, z = ai // 4, ai % 4
    hi, core = ni // 2, ni % 2

    def at(y_=None, z_=None, lo_=None, hi_=None, core_=None):
        pick = lambda new, old: old if new is None else new
        return {"stream": pick(y_, y), "azim": pick(lo_, lo) * 4 + pick(z_, z),
                "normal": pick(hi_, hi) * 2 + pick(core_, core)}

    y_of = lambda d: (y + d) % 4
    z_of = lambda d: (z + d) % 4
    lo_dev = at(lo_=1 - lo)
    hi_dev = at(lo_=1 - lo, hi_=1 - hi)
    core_dev = at(core_=1 - core)
    slot_own = ni
    slot_core = hi * 2 + (1 - core)
    slot_hi = (1 - hi) * 2 + core
    slot_both = (1 - hi) * 2 + (1 - core)

    barrier = pltpu.get_barrier_semaphore()
    partners = [at(y_=y_of(d)) for d in (1, 2, 3)] + [at(z_=z_of(d)) for d in (1, 2, 3)] + [lo_dev, hi_dev, core_dev]
    for device in partners:
        pl.semaphore_signal(barrier, inc=1, device_id=device, device_id_type=MESH)

    def remote(src, dst, key, device):
        i = TABLE[key]
        return pltpu.make_async_remote_copy(src_ref=src, dst_ref=dst, send_sem=ssem.at[i], recv_sem=rsem.at[i],
                                            device_id=device, device_id_type=MESH)

    def zf(t, d):
        return remote(zs.at[2 * z_of(d) + t], gat.at[t, slot_own, z], ("zf", t, d), at(z_=z_of(d)))

    def zb(t, d):
        return remote(zbs.at[2 * z_of(d) + t], zbase.at[t, z], ("zb", t, d), at(z_=z_of(d)))

    def zr(t, d):
        return remote(fz.at[t, z_of(d)], rz.at[2 * z + t], ("zr", t, d), at(z_=z_of(d)))

    def src_own(t, d):
        return zs.at[2 * z + t] if d == 0 else gat.at[t, slot_own, z_of(-d)]

    def lo_c(t, d):
        return remote(src_own(t, d), oth.at[t, z_of(-d)], ("lo", t, d), lo_dev)

    def co(t, d):
        return remote(src_own(t, d), gat.at[t, slot_own, z_of(-d)], ("co", t, d), core_dev)

    def hi_c(t, d):
        return remote(oth.at[t, z_of(-d)], gat.at[t, slot_own, z_of(-d)], ("hi", t, d), hi_dev)

    def cw(t, d):
        return remote(gat.at[t, slot_hi, z_of(-d)], gat.at[t, slot_hi, z_of(-d)], ("cw", t, d), core_dev)

    def yf(g, d):
        return remote(ys.at[y_of(d) * 3 + g], yr.at[g, y], ("yf", g, d), at(y_=y_of(d)))

    def yret(g, d):
        return remote(fy.at[g, y_of(d)], ry.at[y * 3 + g], ("yr", g, d), at(y_=y_of(d)))

    weights = [
        pltpu.make_async_copy(aops.at[k, pl.ds(pl.multiple_of(lo * 512, 512), 512), pl.ds(pl.multiple_of(half * 512, 512), 512)],
                              wa.at[pl.ds(k * 512, 512), pl.ds(j * 512, 512)], lsem.at[2 * k + j])
        for k in range(2) for j, half in enumerate((lo, 1 - lo))
    ]
    for w in weights:
        w.start()

    def lower(st, _):
        zs[st] = pert[:, st].astype(BF16)
        for f in range(4):
            zbs[st, f] = base[1 + f, st]
        return 0

    lax.fori_loop(0, S, lower, 0)
    pl.semaphore_wait(barrier, len(partners))
    for d in (1, 3, 2):
        zf(0, d).start()
    for t in range(2):
        lo_c(t, 0).start()
        co(t, 0).start()
    own = []
    for t in range(2):
        own.append(pltpu.make_async_copy(zs.at[2 * z + t], gat.at[t, slot_own, z], lsem.at[4 + t]))
        own.append(pltpu.make_async_copy(zbs.at[2 * z + t], zbase.at[t, z], lsem.at[6 + t]))
    for c in own:
        c.start()

    def lower_y(i, _):
        rows = pert[:, :, pl.ds(pl.multiple_of(i * 8, 8), 8), :]
        ys[i, 0:NV] = rows.reshape(NV, 64, A).astype(BF16)
        return 0

    lax.fori_loop(0, 12, lower_y, 0)
    for j, f in enumerate((0, 3, 4)):
        wide = base[f].astype(F32)
        for i in range(12):
            ys[i, NV + j] = wide[:, 8 * i:8 * i + 8, :].reshape(64, A).astype(BF16)
    for g in range(3):
        for d in (1, 3, 2):
            yf(g, d).start()
    for d in (1, 3, 2):
        zb(0, d).start()
    for d in (1, 3, 2):
        zf(1, d).start()
    for d in (1, 3, 2):
        zb(1, d).start()
    yown = []
    for g in range(3):
        yown.append(pltpu.make_async_copy(ys.at[y * 3 + g], yr.at[g, y], lsem.at[8 + g]))
    for c in yown:
        c.start()

    ks[...] = spread(sops[...].reshape(64, 32), 8)
    c_high, c_low = split_two(coup[...])
    ky[:, 0:192] = spread(c_high[0], 16)
    ky[:, 192:384] = spread(c_low[0], 16)
    kz[:, 0:192] = spread(c_high[1], 16)
    kz[:, 192:384] = spread(c_high[2], 16)
    kz[:, 384:576] = spread(c_low[1], 16)
    kz[:, 576:768] = spread(c_low[2], 16)
    h_high, h_low = split_two(chem[...])
    for c in range(3):
        high = spread(h_high[c], 16)
        kc[192 * c:192 * c + 192, 0:192] = high
        kc[192 * c:192 * c + 192, 192:384] = high
        kc[192 * c:192 * c + 192, 384:576] = spread(h_low[c], 16)
    for k in range(2):
        kn[96 * k:96 * k + 96] = nops[k, pl.ds(pl.multiple_of(ni * 96, 96), 96), :]

    def scale_of(first_row, rows):
        row = lax.broadcasted_iota(jnp.int32, (rows, A), 0) + first_row + ni * N
        return jnp.where(row == 0, 0.0, 0.2).astype(F32)

    def source(st):
        def pair(q, _):
            r0 = pl.multiple_of(q * 32, 32)
            p = jnp.concatenate([pert[:, st, pl.ds(r0, 16), :].reshape(192, A),
                                 pert[:, st, pl.ds(pl.multiple_of(r0 + 16, 16), 16), :].reshape(192, A)], axis=1)
            high = p.astype(BF16)
            low = (p - high.astype(F32)).astype(BF16)
            parts = jnp.dot(kc[...], jnp.concatenate([high, low, high], axis=0), preferred_element_type=F32)
            parts = parts.reshape(3, NV, 16, 2 * A)
            p = p.reshape(NV, 16, 2 * A)
            for j in range(2):
                rj = pl.multiple_of(r0 + 16 * j, 16)
                lanes = slice(j * A, (j + 1) * A)
                b5, b6, b7 = (base[f, st, pl.ds(rj, 16), :].astype(F32) for f in (5, 6, 7))
                held = scale_of(rj, 16)
                for v in range(NV):
                    here = p[v, :, lanes]
                    src = parts[0, v, :, lanes] + b5 * parts[1, v, :, lanes] + b6 * parts[2, v, :, lanes] - b7 * here
                    out[v, st, pl.ds(rj, 16), :] = here + (held if 5 <= v <= 9 else 0.2) * src
            return 0
        lax.fori_loop(0, 3, pair, 0)

    def sources(first, count):
        def one(i, _):
            source(i)
            return 0
        lax.fori_loop(first, first + count, one, 0)

    def stream_flux(g):
        for d in (1, 3, 2):
            yf(g, d).wait_recv()
        yown[g].wait()

        def derive(q, _):
            x = jnp.concatenate([yr[g, :, 2 * q].reshape(256, A), yr[g, :, 2 * q + 1].reshape(256, A)], axis=1)
            both = jnp.dot(ks[...], x, preferred_element_type=F32)
            for j in range(2):
                dy[0, 2 * q + j] = both[0:256, j * A:(j + 1) * A]
                dy[1, 2 * q + j] = both[256:512, j * A:(j + 1) * A]
            return 0

        lax.fori_loop(0, NV // 2, derive, 0)

        def mix(q, _):
            dst, pr = q // 2, q % 2
            row = lambda j: pl.multiple_of(dst * 64 + pr * 32 + 16 * j, 16)
            first = jnp.concatenate([dy[0, :, pl.ds(row(j), 16), :].reshape(192, A) for j in range(2)], axis=1)
            low = first.astype(BF16)
            mixed = jnp.dot(ky[...], jnp.concatenate([low, low], axis=0), preferred_element_type=F32)
            mixed = mixed.reshape(NV, 16, 2 * A)
            for j in range(2):
                lanes = slice(j * A, (j + 1) * A)
                near = pl.multiple_of(pr * 32 + 16 * j, 16)
                u, rho, nu = (yr[g, dst, NV + f, pl.ds(near, 16), :].astype(F32) for f in range(3))
                for v in range(NV):
                    d1, d2 = dy[0, v, pl.ds(row(j), 16), :], dy[1, v, pl.ds(row(j), 16), :]
                    flux = nu * d2 - u * d1 - rho * mixed[v, :, lanes]
                    fy[g, dst, v, pl.ds(near, 16), :] = flux.astype(BF16)
            return 0

        lax.fori_loop(0, 8, mix, 0)
        for d in (1, 3, 2):
            yret(g, d).start()

    def turned_flux(t):
        def normal(v, _):
            x = jnp.concatenate([gat[t, :, b, v].reshape(384, A) for b in range(4)], axis=1)
            both = jnp.dot(kn[...], x, preferred_element_type=F32)
            dn[0, v] = both[0:96]
            dn[1, v] = both[96:192]
            return 0

        lax.fori_loop(0, NV, normal, 0)

        def rows_of(q, _):
            r = pl.ds(pl.multiple_of(q * 16, 16), 16)
            x = jnp.concatenate([gat[t, slot_own, b, :, r, :].reshape(192, A) for b in range(4)]
                                + [oth[t, b, :, r, :].reshape(192, A) for b in range(4)], axis=1)
            da = lax.dot_general(x, wa[...], (((1,), (1,)), ((), ())), preferred_element_type=F32)
            low_a = da[:, 0:512].astype(BF16)
            low_n = dn[0, :, r, :].reshape(192, 512).astype(BF16)
            mixed = jnp.dot(kz[...], jnp.concatenate([low_a, low_n, low_a, low_n], axis=0), preferred_element_type=F32)
            for b in range(4):
                lanes = slice(b * A, (b + 1) * A)
                u1, u2, rho, nu = (zbase[t, b, f, r, :].astype(F32) for f in range(4))
                for v in range(NV):
                    rv = slice(16 * v, 16 * v + 16)
                    a1, a2 = da[rv, lanes], da[rv, 512 + b * A:512 + (b + 1) * A]
                    n1, n2 = dn[0, v, r, lanes], dn[1, v, r, lanes]
                    flux = nu * (a2 + n2) - u1 * a1 - u2 * n1 - rho * mixed[rv, lanes]
                    fz[t, b, v, r, :] = flux.astype(BF16)
            return 0

        lax.fori_loop(0, N // 16, rows_of, 0)
        for d in (1, 3, 2):
            zr(t, d).start()

    def pass_lo(t, d):
        zf(t, d).wait_recv()
        lo_c(t, d).start()
        co(t, d).start()

    def pass_hi(t, d):
        lo_c(t, d).wait_recv()
        hi_c(t, d).start()

    def pass_core(t, d):
        hi_c(t, d).wait_recv()
        cw(t, d).start()

    def wait_station(t):
        for d in range(4):
            co(t, d).wait_recv()
            cw(t, d).wait_recv()
        for d in (1, 2, 3):
            zb(t, d).wait_recv()
        own[2 * t].wait()
        own[2 * t + 1].wait()

    def add_stream(g, d):
        i = y_of(-d) * 3 + g
        r = pl.ds(pl.multiple_of(i * 8, 8), 8)
        held = scale_of(i * 8, 8)
        for v in range(NV):
            src = fy[g, y, v] if d == 0 else ry[i, v]
            out[v, :, r, :] += (held if 5 <= v <= 9 else 0.2) * src.astype(F32).reshape(S, 8, A)

    def add_turned(t, d):
        st = 2 * z_of(-d) + t
        held = scale_of(0, N)
        for v in range(NV):
            src = fz[t, z, v] if d == 0 else rz[st, v]
            out[v, st] += (held if 5 <= v <= 9 else 0.2) * src.astype(F32)

    sources(0, 2)
    pass_hi(0, 0)
    sources(2, 1)
    pass_lo(0, 1)
    pass_lo(0, 3)
    stream_flux(0)
    pass_hi(1, 0)
    pass_core(0, 0)
    sources(3, 1)
    pass_lo(0, 2)
    pass_hi(0, 1)
    pass_core(1, 0)
    stream_flux(1)
    pass_hi(0, 3)
    pass_core(0, 1)
    sources(4, 1)
    pass_lo(1, 1)
    pass_lo(1, 3)
    pass_hi(0, 2)
    pass_core(0, 3)
    stream_flux(2)
    pass_lo(1, 2)
    sources(5, 3)
    pass_hi(1, 1)
    pass_core(0, 2)
    for w in weights:
        w.wait()
    wait_station(0)
    turned_flux(0)
    pass_hi(1, 3)
    pass_core(1, 1)
    for g in range(2):
        add_stream(g, 0)
        for d in (1, 3, 2):
            yret(g, d).wait_recv()
            add_stream(g, d)
    pass_hi(1, 2)
    pass_core(1, 3)
    add_stream(2, 0)
    for d in (1, 3, 2):
        yret(2, d).wait_recv()
        add_stream(2, d)
    pass_core(1, 2)
    wait_station(1)
    turned_flux(1)
    for t in range(2):
        add_turned(t, 0)
        for d in (1, 3, 2):
            zr(t, d).wait_recv()
            add_turned(t, d)
    for t in range(2):
        for d in range(4):
            for copy in (lo_c, co, hi_c, cw):
                copy(t, d).wait_send()
        for d in (1, 2, 3):
            for copy in (zf, zb, zr):
                copy(t, d).wait_send()
    for g in range(3):
        for d in (1, 2, 3):
            yf(g, d).wait_send()
            yret(g, d).wait_send()


def shards(perturbation, base_flow, stream_ops, azimuth_ops, normal_ops, coupling, chemistry):
    vmem = pl.BlockSpec(memory_space=pltpu.VMEM)
    scratch = lambda *shape: pltpu.VMEM(shape, BF16)
    return pl.pallas_call(
        kernel,
        out_shape=jax.ShapeDtypeStruct(perturbation.shape, F32),
        in_specs=[vmem, vmem, vmem, pl.BlockSpec(memory_space=pl.ANY), vmem, vmem, vmem],
        out_specs=vmem,
        scratch_shapes=[
            scratch(S, NV, N, A),
            scratch(S, 4, N, A),
            scratch(2, 4, 4, NV, N, A),
            scratch(2, 4, 4, N, A),
            scratch(2, 4, NV, N, A),
            scratch(12, 15, 64, A),
            scratch(3, 4, 15, 64, A),
            scratch(3, 4, NV, 64, A),
            scratch(12, NV, 64, A),
            scratch(2, 4, NV, N, A),
            scratch(S, NV, N, A),
            pltpu.VMEM((2, NV, N, 512), F32),
            pltpu.VMEM((2, NV, 256, A), F32),
            scratch(1024, 1024),
            scratch(576, 576),
            scratch(192, 384),
            scratch(192, 768),
            scratch(512, 256),
            scratch(192, 384),
            pltpu.SemaphoreType.DMA((COPIES,)),
            pltpu.SemaphoreType.DMA((COPIES,)),
            pltpu.SemaphoreType.DMA((11,)),
        ],
        compiler_params=pltpu.CompilerParams(collective_id=0, has_side_effects=True, vmem_limit_bytes=62 << 20),
    )(perturbation, base_flow, stream_ops, azimuth_ops, normal_ops, coupling, chemistry)


def solution(mesh):
    field = P(None, "stream", "normal", "azim")
    return jax.shard_map(
        shards,
        mesh=mesh,
        in_specs=(field, field, P(), P(), P(), P(), P()),
        out_specs=field,
        check_vma=False,
    )
```

time: 643 us -> 116 us (0.18)
  local copies, waits for them, and re-layouts: 353 us -> 4.84 us
  Pallas kernels: 0 us -> 111 us
  matrix products: 82.2 us -> 0 us
  waiting for transfers between devices: 74.3 us -> 0 us
  other arithmetic: 64.1 us -> 0 us
  starting transfers between devices: 43.9 us -> 0 us
  blocking collectives: 18.2 us -> 0 us
    unnamed x40 -> x1, local copies, waits for them, and re-layouts: 197 us -> 4.84 us
    pallas_call x0 -> x1, Pallas kernels: none -> 111 us  [shards(): pl.pallas_call(kernel, out_shape=jax.ShapeDtypeStruct(perturbation.shape,...]
    dot_general x10 -> x0, matrix products: 82.2 us -> none  [the longest x3 31.1 us: flux_terms(): jnp.einsum('vw,wxyz->vxyz', coupling_d, first_der, precision=highest)]
    all_to_all x13 -> x0, local copies, waits for them, and re-layouts: 82.1 us -> none  [the longest x1 30.6 us: shards(): lax.all_to_all(azim_terms, 'azim', split_axis=3, concat_axis=2, tiled=True)]
    all_to_all x8 -> x0, waiting for transfers between devices: 74.3 us -> none  [the longest x1 35.6 us: shards(): lax.all_to_all(lowered, 'normal', split_axis=3, concat_axis=2, tiled=True)]
    add x3 -> x0, local copies, waits for them, and re-layouts: 60.4 us -> none  [flux_terms(): -velocity.astype(jnp.float32) * first_der]
    all_to_all x8 -> x0, starting transfers between devices: 43.9 us -> none  [the longest x1 7.83 us: shards(): lax.all_to_all(lowered, 'normal', split_axis=3, concat_axis=2, tiled=True)]
    all_to_all x2 -> x0, other arithmetic: 33.7 us -> none  [the longest x1 17.5 us: shards(): lax.all_to_all(jnp.swapaxes(normal_terms, 2, 3), 'normal', split_axis=2,...]
  transfers between devices with their start and end apart: 8 -> 0, of which waited for: 5 -> 0; matrix products, arithmetic and copies ran while one was open for 54% -> 0% of each run, Pallas kernels for 0% -> 0%
where the time goes in v1:
time: 116 us
  Pallas kernels  111 us (96%)
  local copies, waits for them, and re-layouts  4.84 us (4%)
    pallas_call x1, Pallas kernels, shards(): pl.pallas_call(kernel, out_shape=jax.ShapeDtypeStruct(perturbation.shape,...  111 us
    unnamed x1, local copies, waits for them, and re-layouts  4.84 us

profile of v1, /device:TPU:1, one launch (start us, length us, event | category | flops | bytes accessed | tf_op | source)
XLA Modules:
  0.0 115.7 jit_solution(18155853948610784368)
XLA Ops:
  0.0 110.9 %shard_map.73 = f32[12,8,96,128]{3,2,1,0:T(8,128)} custom-call(f32[12,8,96,128]{3,2,1,0:T(8,128)} %pert.1, bf16[8,8,96,128]{3,2,1,0:T(8,128)(2,1)} %base.1, bf16[2,32,32]{2,1,0:T(8,128)(2,1)} %sops.1, bf16[2,1024,1024]{2,1,0:T(8,128)(2,1)} %aops.1, bf16[2,384,384]{2,1,0:T(8,128)(2,1)} %nops.1, f32[3,12,12]{2,1,0:T(8,128)} %coup.1, f32[3,12,12]{2,1,0:T(8,128)} %chem.1), custom_call_target="tpu_custom_call" | custom-call | tf_op jit(solution)/shard_map/pallas_call | solution.py:394
  110.9 4.8 %copy.9 = f32[12,8,96,128]{3,2,1,0:T(8,128)} copy(f32[12,8,96,128]{3,2,1,0:T(8,128)} %shard_map.73) | data formatting | bytes 9437184

commit v2 on v1

--- a/solution.py
+++ b/solution.py
@@ -53,9 +53,14 @@
     return high, (matrix - high.astype(F32)).astype(BF16)
 
 
-def kernel(pert, base, sops, aops, nops, coup, chem, out,
-           zs, zbs, gat, zbase, oth, ys, yr, fy, ry, fz, rz, dn, dy, wa, kc, ky, kz, ks, kn,
-           ssem, rsem, lsem):
+def kernel(pert_hbm, base_hbm, sops, aops, nops, coup, chem, out_hbm,
+           pert, base, out, zs, zbs, gat, zbase, oth, ys, yr, fy, ry, fz, rz, da, dn, dy, wa, kc, ky, kz, ks, kn,
+           ssem, rsem, lsem, isem, wsem, osem):
+    loads = [(pltpu.make_async_copy(pert_hbm.at[:, st], pert.at[:, st], isem.at[2 * st]),
+              pltpu.make_async_copy(base_hbm.at[:, st], base.at[:, st], isem.at[2 * st + 1])) for st in range(S)]
+    for pair in loads:
+        for load in pair:
+            load.start()
     y = lax.axis_index("stream")
     ai = lax.axis_index("azim")
     ni = lax.axis_index("normal")
@@ -117,21 +122,12 @@
     def yret(g, d):
         return remote(fy.at[g, y_of(d)], ry.at[y * 3 + g], ("yr", g, d), at(y_=y_of(d)))
 
-    weights = [
-        pltpu.make_async_copy(aops.at[k, pl.ds(pl.multiple_of(lo * 512, 512), 512), pl.ds(pl.multiple_of(half * 512, 512), 512)],
-                              wa.at[pl.ds(k * 512, 512), pl.ds(j * 512, 512)], lsem.at[2 * k + j])
-        for k in range(2) for j, half in enumerate((lo, 1 - lo))
-    ]
-    for w in weights:
-        w.start()
-
-    def lower(st, _):
+    for st in range(S):
+        for load in loads[st]:
+            load.wait()
         zs[st] = pert[:, st].astype(BF16)
         for f in range(4):
             zbs[st, f] = base[1 + f, st]
-        return 0
-
-    lax.fori_loop(0, S, lower, 0)
     pl.semaphore_wait(barrier, len(partners))
     for d in (1, 3, 2):
         zf(0, d).start()
@@ -169,6 +165,14 @@
         yown.append(pltpu.make_async_copy(ys.at[y * 3 + g], yr.at[g, y], lsem.at[8 + g]))
     for c in yown:
         c.start()
+    weights = [
+        pltpu.make_async_copy(
+            aops.at[k, pl.ds(pl.multiple_of(lo * 512, 512), 512), pl.ds(pl.multiple_of(half * 512 + b * A, A), A)],
+            wa.at[j, b, pl.ds(k * 512, 512)], wsem.at[8 * k + 4 * j + b])
+        for k in range(2) for j, half in enumerate((lo, 1 - lo)) for b in range(4)
+    ]
+    for w in weights:
+        w.start()
 
     ks[...] = spread(sops[...].reshape(64, 32), 8)
     c_high, c_low = split_two(coup[...])
@@ -255,38 +259,58 @@
         for d in (1, 3, 2):
             yret(g, d).start()
 
-    def turned_flux(t):
-        def normal(v, _):
-            x = jnp.concatenate([gat[t, :, b, v].reshape(384, A) for b in range(4)], axis=1)
-            both = jnp.dot(kn[...], x, preferred_element_type=F32)
-            dn[0, v] = both[0:96]
-            dn[1, v] = both[96:192]
-            return 0
-
-        lax.fori_loop(0, NV, normal, 0)
-
+    def azimuth(t, own_blocks, other_blocks, fresh):
         def rows_of(q, _):
             r = pl.ds(pl.multiple_of(q * 16, 16), 16)
-            x = jnp.concatenate([gat[t, slot_own, b, :, r, :].reshape(192, A) for b in range(4)]
-                                + [oth[t, b, :, r, :].reshape(192, A) for b in range(4)], axis=1)
-            da = lax.dot_general(x, wa[...], (((1,), (1,)), ((), ())), preferred_element_type=F32)
-            low_a = da[:, 0:512].astype(BF16)
-            low_n = dn[0, :, r, :].reshape(192, 512).astype(BF16)
+            x = [gat[t, slot_own, b, :, r, :].reshape(192, A) for b in own_blocks]
+            x += [oth[t, b, :, r, :].reshape(192, A) for b in other_blocks]
+            w = [wa[0, b] for b in own_blocks] + [wa[1, b] for b in other_blocks]
+            both = lax.dot_general(jnp.concatenate(x, axis=1), jnp.concatenate(w, axis=1), (((1,), (1,)), ((), ())),
+                                   preferred_element_type=F32)
+            for k in range(2):
+                for b in range(4):
+                    part = both[:, k * 512 + b * A:k * 512 + (b + 1) * A].reshape(NV, 16, A)
+                    if not fresh:
+                        part = part + da[k, b, :, r, :]
+                    da[k, b, :, r, :] = part
+            return 0
+
+        lax.fori_loop(0, N // 16, rows_of, 0)
+
+    def turned_flux(t, d):
+        b = z_of(-d)
+        co(t, d).wait_recv()
+        cw(t, d).wait_recv()
+        if d:
+            zb(t, d).wait_recv()
+
+        def normal(q, _):
+            x = jnp.concatenate([gat[t, :, b, 2 * q].reshape(384, A), gat[t, :, b, 2 * q + 1].reshape(384, A)], axis=1)
+            both = jnp.dot(kn[...], x, preferred_element_type=F32)
+            for j in range(2):
+                for k in range(2):
+                    dn[k, 2 * q + j] = both[96 * k:96 * k + 96, j * A:(j + 1) * A]
+            return 0
+
+        lax.fori_loop(0, NV // 2, normal, 0)
+
+        def mix(q, _):
+            rs = [pl.ds(pl.multiple_of(q * 32 + 16 * j, 16), 16) for j in range(2)]
+            low_a = jnp.concatenate([da[0, b, :, r, :].reshape(192, A) for r in rs], axis=1).astype(BF16)
+            low_n = jnp.concatenate([dn[0, :, r, :].reshape(192, A) for r in rs], axis=1).astype(BF16)
             mixed = jnp.dot(kz[...], jnp.concatenate([low_a, low_n, low_a, low_n], axis=0), preferred_element_type=F32)
-            for b in range(4):
-                lanes = slice(b * A, (b + 1) * A)
+            for j, r in enumerate(rs):
+                lanes = slice(j * A, (j + 1) * A)
                 u1, u2, rho, nu = (zbase[t, b, f, r, :].astype(F32) for f in range(4))
                 for v in range(NV):
-                    rv = slice(16 * v, 16 * v + 16)
-                    a1, a2 = da[rv, lanes], da[rv, 512 + b * A:512 + (b + 1) * A]
-                    n1, n2 = dn[0, v, r, lanes], dn[1, v, r, lanes]
-                    flux = nu * (a2 + n2) - u1 * a1 - u2 * n1 - rho * mixed[rv, lanes]
+                    flux = (nu * (da[1, b, v, r, :] + dn[1, v, r, :]) - u1 * da[0, b, v, r, :] - u2 * dn[0, v, r, :]
+                            - rho * mixed[16 * v:16 * v + 16, lanes])
                     fz[t, b, v, r, :] = flux.astype(BF16)
             return 0
 
-        lax.fori_loop(0, N // 16, rows_of, 0)
-        for d in (1, 3, 2):
-            zr(t, d).start()
+        lax.fori_loop(0, N // 32, mix, 0)
+        if d:
+            zr(t, 4 - d).start()
 
     def pass_lo(t, d):
         zf(t, d).wait_recv()
@@ -300,15 +324,6 @@
     def pass_core(t, d):
         hi_c(t, d).wait_recv()
         cw(t, d).start()
-
-    def wait_station(t):
-        for d in range(4):
-            co(t, d).wait_recv()
-            cw(t, d).wait_recv()
-        for d in (1, 2, 3):
-            zb(t, d).wait_recv()
-        own[2 * t].wait()
-        own[2 * t + 1].wait()
 
     def add_stream(g, d):
         i = y_of(-d) * 3 + g
@@ -324,57 +339,73 @@
         for v in range(NV):
             src = fz[t, z, v] if d == 0 else rz[st, v]
             out[v, st] += (held if 5 <= v <= 9 else 0.2) * src.astype(F32)
+        store(t, d).start()
+
+    def store(t, d):
+        st = 2 * z_of(-d) + t
+        return pltpu.make_async_copy(out.at[:, st], out_hbm.at[:, st], osem.at[4 * t + d])
 
     sources(0, 2)
     pass_hi(0, 0)
     sources(2, 1)
     pass_lo(0, 1)
     pass_lo(0, 3)
-    stream_flux(0)
+    sources(3, 1)
     pass_hi(1, 0)
     pass_core(0, 0)
-    sources(3, 1)
+    sources(4, 1)
     pass_lo(0, 2)
+    sources(5, 1)
     pass_hi(0, 1)
     pass_core(1, 0)
-    stream_flux(1)
+    stream_flux(0)
+    sources(6, 1)
     pass_hi(0, 3)
     pass_core(0, 1)
-    sources(4, 1)
+    sources(7, 1)
     pass_lo(1, 1)
     pass_lo(1, 3)
+    for w in weights:
+        w.wait()
+    for c in own:
+        c.wait()
     pass_hi(0, 2)
     pass_core(0, 3)
-    stream_flux(2)
     pass_lo(1, 2)
-    sources(5, 3)
+    azimuth(0, range(4), range(4), True)
+    stream_flux(1)
     pass_hi(1, 1)
     pass_core(0, 2)
-    for w in weights:
-        w.wait()
-    wait_station(0)
-    turned_flux(0)
+    for d in (1, 3, 0):
+        turned_flux(0, d)
+    stream_flux(2)
+    turned_flux(0, 2)
     pass_hi(1, 3)
     pass_core(1, 1)
-    for g in range(2):
-        add_stream(g, 0)
+    azimuth(1, range(4), [z_of(-d) for d in (0, 1, 3)], True)
+    add_stream(0, 0)
+    pass_hi(1, 2)
+    pass_core(1, 3)
+    azimuth(1, [], [z_of(-2)], False)
+    turned_flux(1, 1)
+    turned_flux(1, 3)
+    pass_core(1, 2)
+    turned_flux(1, 2)
+    turned_flux(1, 0)
+    for g in range(3):
+        if g:
+            add_stream(g, 0)
         for d in (1, 3, 2):
             yret(g, d).wait_recv()
             add_stream(g, d)
-    pass_hi(1, 2)
-    pass_core(1, 3)
-    add_stream(2, 0)
-    for d in (1, 3, 2):
-        yret(2, d).wait_recv()
-        add_stream(2, d)
-    pass_core(1, 2)
-    wait_station(1)
-    turned_flux(1)
-    for t in range(2):
-        add_turned(t, 0)
-        for d in (1, 3, 2):
-            zr(t, d).wait_recv()
+    for t in range(2):
+        for d in (0, 1, 3, 2):
+            if d:
+                zr(t, d).wait_recv()
             add_turned(t, d)
+    for t in range(2):
+        for d in range(4):
+            store(t, d).wait()
     for t in range(2):
         for d in range(4):
             for copy in (lo_c, co, hi_c, cw):
@@ -390,13 +421,17 @@
 
 def shards(perturbation, base_flow, stream_ops, azimuth_ops, normal_ops, coupling, chemistry):
     vmem = pl.BlockSpec(memory_space=pltpu.VMEM)
+    hbm = pl.BlockSpec(memory_space=pl.ANY)
     scratch = lambda *shape: pltpu.VMEM(shape, BF16)
     return pl.pallas_call(
         kernel,
         out_shape=jax.ShapeDtypeStruct(perturbation.shape, F32),
-        in_specs=[vmem, vmem, vmem, pl.BlockSpec(memory_space=pl.ANY), vmem, vmem, vmem],
-        out_specs=vmem,
+        in_specs=[hbm, hbm, vmem, hbm, vmem, vmem, vmem],
+        out_specs=hbm,
         scratch_shapes=[
+            pltpu.VMEM((NV, S, N, A), F32),
+            scratch(8, S, N, A),
+            pltpu.VMEM((NV, S, N, A), F32),
             scratch(S, NV, N, A),
             scratch(S, 4, N, A),
             scratch(2, 4, 4, NV, N, A),
@@ -408,9 +443,10 @@
             scratch(12, NV, 64, A),
             scratch(2, 4, NV, N, A),
             scratch(S, NV, N, A),
-            pltpu.VMEM((2, NV, N, 512), F32),
+            pltpu.VMEM((2, 4, NV, N, A), F32),
+            pltpu.VMEM((2, NV, N, A), F32),
             pltpu.VMEM((2, NV, 256, A), F32),
-            scratch(1024, 1024),
+            scratch(2, 4, 1024, A),
             scratch(576, 576),
             scratch(192, 384),
             scratch(192, 768),
@@ -419,6 +455,9 @@
             pltpu.SemaphoreType.DMA((COPIES,)),
             pltpu.SemaphoreType.DMA((COPIES,)),
             pltpu.SemaphoreType.DMA((11,)),
+            pltpu.SemaphoreType.DMA((2 * S,)),
+            pltpu.SemaphoreType.DMA((16,)),
+            pltpu.SemaphoreType.DMA((8,)),
         ],
         compiler_params=pltpu.CompilerParams(collective_id=0, has_side_effects=True, vmem_limit_bytes=62 << 20),
     )(perturbation, base_flow, stream_ops, azimuth_ops, normal_ops, coupling, chemistry)

time: 116 us -> 99.1 us (0.85)
  Pallas kernels: 111 us -> 94.1 us
    pallas_call x1, Pallas kernels: 111 us -> 94.1 us  [shards(): pl.pallas_call(kernel, out_shape=jax.ShapeDtypeStruct(perturbation.shape,...]
where the time goes in v2:
time: 99.1 us; the launch traced here: 98.9 us
  Pallas kernels  94.1 us (95%)
  local copies, waits for them, and re-layouts  4.84 us (5%)
    pallas_call x1, Pallas kernels, shards(): pl.pallas_call(kernel, out_shape=jax.ShapeDtypeStruct(perturbation.shape,...  94.1 us
    unnamed x1, local copies, waits for them, and re-layouts  4.84 us

profile of v2, /device:TPU:1, one launch (start us, length us, event | category | flops | bytes accessed | tf_op | source)
XLA Modules:
  0.0 98.9 jit_solution(8486911197268097713)
XLA Ops:
  0.0 94.1 %shard_map.73 = f32[12,8,96,128]{3,2,1,0:T(8,128)} custom-call(f32[12,8,96,128]{3,2,1,0:T(8,128)} %pert_hbm.1, bf16[8,8,96,128]{3,2,1,0:T(8,128)(2,1)} %base_hbm.1, bf16[2,32,32]{2,1,0:T(8,128)(2,1)} %sops.1, bf16[2,1024,1024]{2,1,0:T(8,128)(2,1)} %aops.1, bf16[2,384,384]{2,1,0:T(8,128)(2,1)} %nops.1, f32[3,12,12]{2,1,0:T(8,128)} %coup.1, f32[3,12,12]{2,1,0:T(8,128)} %chem.1), custom_call_target="tpu_custom_call" | custom-call | tf_op jit(solution)/shard_map/pallas_call | solution.py:426
  94.1 4.8 %copy.9 = f32[12,8,96,128]{3,2,1,0:T(8,128)} copy(f32[12,8,96,128]{3,2,1,0:T(8,128)} %shard_map.73) | data formatting | bytes 9437184

commit v3 on v2

--- a/solution.py
+++ b/solution.py
@@ -53,14 +53,9 @@
     return high, (matrix - high.astype(F32)).astype(BF16)
 
 
-def kernel(pert_hbm, base_hbm, sops, aops, nops, coup, chem, out_hbm,
-           pert, base, out, zs, zbs, gat, zbase, oth, ys, yr, fy, ry, fz, rz, da, dn, dy, wa, kc, ky, kz, ks, kn,
-           ssem, rsem, lsem, isem, wsem, osem):
-    loads = [(pltpu.make_async_copy(pert_hbm.at[:, st], pert.at[:, st], isem.at[2 * st]),
-              pltpu.make_async_copy(base_hbm.at[:, st], base.at[:, st], isem.at[2 * st + 1])) for st in range(S)]
-    for pair in loads:
-        for load in pair:
-            load.start()
+def kernel(pert_hbm, base_hbm, sops, aops, nops, coup, chem, out,
+           pert, base, zs, zbs, gat, zbase, oth, ys, yr, fy, ry, fz, rz, da, dn, dy, wa, kc, ky, kz, ks, kn,
+           ssem, rsem, lsem, isem, wsem):
     y = lax.axis_index("stream")
     ai = lax.axis_index("azim")
     ni = lax.axis_index("normal")
@@ -82,6 +77,13 @@
     slot_hi = (1 - hi) * 2 + core
     slot_both = (1 - hi) * 2 + (1 - core)
 
+    stations = [2 * z_of(d) + t for t in range(2) for d in (0, 1, 3, 2)]
+    loads = [(pltpu.make_async_copy(pert_hbm.at[:, st], pert.at[:, st], isem.at[2 * i]),
+              pltpu.make_async_copy(base_hbm.at[:, st], base.at[:, st], isem.at[2 * i + 1]))
+             for i, st in enumerate(stations)]
+    for pair in loads:
+        for load in pair:
+            load.start()
     barrier = pltpu.get_barrier_semaphore()
     partners = [at(y_=y_of(d)) for d in (1, 2, 3)] + [at(z_=z_of(d)) for d in (1, 2, 3)] + [lo_dev, hi_dev, core_dev]
     for device in partners:
@@ -122,18 +124,26 @@
     def yret(g, d):
         return remote(fy.at[g, y_of(d)], ry.at[y * 3 + g], ("yr", g, d), at(y_=y_of(d)))
 
-    for st in range(S):
-        for load in loads[st]:
+    def lower(i):
+        for load in loads[i]:
             load.wait()
+        st = stations[i]
         zs[st] = pert[:, st].astype(BF16)
         for f in range(4):
             zbs[st, f] = base[1 + f, st]
+
+    lower(0)
     pl.semaphore_wait(barrier, len(partners))
-    for d in (1, 3, 2):
+    lo_c(0, 0).start()
+    co(0, 0).start()
+    for i, d in enumerate((1, 3, 2)):
+        lower(1 + i)
         zf(0, d).start()
-    for t in range(2):
-        lo_c(t, 0).start()
-        co(t, 0).start()
+    lower(4)
+    lo_c(1, 0).start()
+    co(1, 0).start()
+    for i in (5, 6, 7):
+        lower(i)
     own = []
     for t in range(2):
         own.append(pltpu.make_async_copy(zs.at[2 * z + t], gat.at[t, slot_own, z], lsem.at[4 + t]))
@@ -215,7 +225,7 @@
                     src = parts[0, v, :, lanes] + b5 * parts[1, v, :, lanes] + b6 * parts[2, v, :, lanes] - b7 * here
                     out[v, st, pl.ds(rj, 16), :] = here + (held if 5 <= v <= 9 else 0.2) * src
             return 0
-        lax.fori_loop(0, 3, pair, 0)
+        lax.fori_loop(0, 3, pair, 0, unroll=3)
 
     def sources(first, count):
         def one(i, _):
@@ -236,7 +246,7 @@
                 dy[1, 2 * q + j] = both[256:512, j * A:(j + 1) * A]
             return 0
 
-        lax.fori_loop(0, NV // 2, derive, 0)
+        lax.fori_loop(0, NV // 2, derive, 0, unroll=6)
 
         def mix(q, _):
             dst, pr = q // 2, q % 2
@@ -255,7 +265,7 @@
                     fy[g, dst, v, pl.ds(near, 16), :] = flux.astype(BF16)
             return 0
 
-        lax.fori_loop(0, 8, mix, 0)
+        lax.fori_loop(0, 8, mix, 0, unroll=2)
         for d in (1, 3, 2):
             yret(g, d).start()
 
@@ -271,11 +281,11 @@
                 for b in range(4):
                     part = both[:, k * 512 + b * A:k * 512 + (b + 1) * A].reshape(NV, 16, A)
                     if not fresh:
-                        part = part + da[k, b, :, r, :]
-                    da[k, b, :, r, :] = part
-            return 0
-
-        lax.fori_loop(0, N // 16, rows_of, 0)
+                        part = part + da[t, k, b, :, r, :]
+                    da[t, k, b, :, r, :] = part
+            return 0
+
+        lax.fori_loop(0, N // 16, rows_of, 0, unroll=2)
 
     def turned_flux(t, d):
         b = z_of(-d)
@@ -292,23 +302,23 @@
                     dn[k, 2 * q + j] = both[96 * k:96 * k + 96, j * A:(j + 1) * A]
             return 0
 
-        lax.fori_loop(0, NV // 2, normal, 0)
+        lax.fori_loop(0, NV // 2, normal, 0, unroll=6)
 
         def mix(q, _):
             rs = [pl.ds(pl.multiple_of(q * 32 + 16 * j, 16), 16) for j in range(2)]
-            low_a = jnp.concatenate([da[0, b, :, r, :].reshape(192, A) for r in rs], axis=1).astype(BF16)
+            low_a = jnp.concatenate([da[t, 0, b, :, r, :].reshape(192, A) for r in rs], axis=1).astype(BF16)
             low_n = jnp.concatenate([dn[0, :, r, :].reshape(192, A) for r in rs], axis=1).astype(BF16)
             mixed = jnp.dot(kz[...], jnp.concatenate([low_a, low_n, low_a, low_n], axis=0), preferred_element_type=F32)
             for j, r in enumerate(rs):
                 lanes = slice(j * A, (j + 1) * A)
                 u1, u2, rho, nu = (zbase[t, b, f, r, :].astype(F32) for f in range(4))
                 for v in range(NV):
-                    flux = (nu * (da[1, b, v, r, :] + dn[1, v, r, :]) - u1 * da[0, b, v, r, :] - u2 * dn[0, v, r, :]
+                    flux = (nu * (da[t, 1, b, v, r, :] + dn[1, v, r, :]) - u1 * da[t, 0, b, v, r, :] - u2 * dn[0, v, r, :]
                             - rho * mixed[16 * v:16 * v + 16, lanes])
                     fz[t, b, v, r, :] = flux.astype(BF16)
             return 0
 
-        lax.fori_loop(0, N // 32, mix, 0)
+        lax.fori_loop(0, N // 32, mix, 0, unroll=3)
         if d:
             zr(t, 4 - d).start()
 
@@ -339,62 +349,50 @@
         for v in range(NV):
             src = fz[t, z, v] if d == 0 else rz[st, v]
             out[v, st] += (held if 5 <= v <= 9 else 0.2) * src.astype(F32)
-        store(t, d).start()
-
-    def store(t, d):
-        st = 2 * z_of(-d) + t
-        return pltpu.make_async_copy(out.at[:, st], out_hbm.at[:, st], osem.at[4 * t + d])
-
-    sources(0, 2)
-    pass_hi(0, 0)
-    sources(2, 1)
-    pass_lo(0, 1)
-    pass_lo(0, 3)
-    sources(3, 1)
-    pass_hi(1, 0)
-    pass_core(0, 0)
-    sources(4, 1)
-    pass_lo(0, 2)
-    sources(5, 1)
-    pass_hi(0, 1)
-    pass_core(1, 0)
+
+    order = [(0, 0), (1, 0), (0, 1), (0, 3), (0, 2), (1, 1), (1, 3), (1, 2)]
+
+    def step(k):
+        pass_hi(*order[k])
+        if k + 2 < 8:
+            pass_lo(*order[k + 2])
+        if 2 <= k < 7:
+            pass_core(*order[k - 2])
+
+    sources(0, 3)
+    step(0)
+    sources(3, 3)
+    step(1)
+    sources(6, 2)
+    step(2)
     stream_flux(0)
-    sources(6, 1)
-    pass_hi(0, 3)
-    pass_core(0, 1)
-    sources(7, 1)
-    pass_lo(1, 1)
-    pass_lo(1, 3)
+    step(3)
+    stream_flux(1)
     for w in weights:
         w.wait()
     for c in own:
         c.wait()
-    pass_hi(0, 2)
-    pass_core(0, 3)
-    pass_lo(1, 2)
+    step(4)
     azimuth(0, range(4), range(4), True)
-    stream_flux(1)
-    pass_hi(1, 1)
-    pass_core(0, 2)
-    for d in (1, 3, 0):
-        turned_flux(0, d)
     stream_flux(2)
+    step(5)
+    turned_flux(0, 0)
+    turned_flux(0, 1)
+    azimuth(1, range(4), [z_of(-d) for d in (0, 1)], True)
+    step(6)
+    turned_flux(0, 3)
     turned_flux(0, 2)
-    pass_hi(1, 3)
     pass_core(1, 1)
-    azimuth(1, range(4), [z_of(-d) for d in (0, 1, 3)], True)
-    add_stream(0, 0)
-    pass_hi(1, 2)
+    step(7)
+    azimuth(1, [], [z_of(-d) for d in (3, 2)], False)
+    turned_flux(1, 1)
     pass_core(1, 3)
-    azimuth(1, [], [z_of(-2)], False)
-    turned_flux(1, 1)
     turned_flux(1, 3)
+    turned_flux(1, 0)
     pass_core(1, 2)
     turned_flux(1, 2)
-    turned_flux(1, 0)
     for g in range(3):
-        if g:
-            add_stream(g, 0)
+        add_stream(g, 0)
         for d in (1, 3, 2):
             yret(g, d).wait_recv()
             add_stream(g, d)
@@ -403,9 +401,6 @@
             if d:
                 zr(t, d).wait_recv()
             add_turned(t, d)
-    for t in range(2):
-        for d in range(4):
-            store(t, d).wait()
     for t in range(2):
         for d in range(4):
             for copy in (lo_c, co, hi_c, cw):
@@ -425,13 +420,12 @@
     scratch = lambda *shape: pltpu.VMEM(shape, BF16)
     return pl.pallas_call(
         kernel,
-        out_shape=jax.ShapeDtypeStruct(perturbation.shape, F32),
+        out_shape=pltpu.VMEM(perturbation.shape, F32),
         in_specs=[hbm, hbm, vmem, hbm, vmem, vmem, vmem],
-        out_specs=hbm,
+        out_specs=vmem,
         scratch_shapes=[
             pltpu.VMEM((NV, S, N, A), F32),
             scratch(8, S, N, A),
-            pltpu.VMEM((NV, S, N, A), F32),
             scratch(S, NV, N, A),
             scratch(S, 4, N, A),
             scratch(2, 4, 4, NV, N, A),
@@ -443,7 +437,7 @@
             scratch(12, NV, 64, A),
             scratch(2, 4, NV, N, A),
             scratch(S, NV, N, A),
-            pltpu.VMEM((2, 4, NV, N, A), F32),
+            pltpu.VMEM((2, 2, 4, NV, N, A), F32),
             pltpu.VMEM((2, NV, N, A), F32),
             pltpu.VMEM((2, NV, 256, A), F32),
             scratch(2, 4, 1024, A),
@@ -457,9 +451,8 @@
             pltpu.SemaphoreType.DMA((11,)),
             pltpu.SemaphoreType.DMA((2 * S,)),
             pltpu.SemaphoreType.DMA((16,)),
-            pltpu.SemaphoreType.DMA((8,)),
         ],
-        compiler_params=pltpu.CompilerParams(collective_id=0, has_side_effects=True, vmem_limit_bytes=62 << 20),
+        compiler_params=pltpu.CompilerParams(collective_id=0, has_side_effects=True, vmem_limit_bytes=56 << 20),
     )(perturbation, base_flow, stream_ops, azimuth_ops, normal_ops, coupling, chemistry)
 
 

time: 99.1 us -> 86.4 us (0.87)
  Pallas kernels: 94.1 us -> 84.1 us
  local copies, waits for them, and re-layouts: 4.84 us -> 2.19 us
    pallas_call x1, Pallas kernels: 94.1 us -> 84.1 us  [shards(): pl.pallas_call(kernel, out_shape=pltpu.VMEM(perturbation.shape, F32), in_...]
    unnamed x1, local copies, waits for them, and re-layouts: 4.84 us -> 2.19 us
where the time goes in v3:
time: 86.4 us; the launch traced here: 86.3 us
  Pallas kernels  84.1 us (97%)
  local copies, waits for them, and re-layouts  2.19 us (3%)
    pallas_call x1, Pallas kernels, shards(): pl.pallas_call(kernel, out_shape=pltpu.VMEM(perturbation.shape, F32), in_...  84.1 us
    unnamed x1, local copies, waits for them, and re-layouts  2.19 us

profile of v3, /device:TPU:1, one launch (start us, length us, event | category | flops | bytes accessed | tf_op | source)
XLA Modules:
  0.0 86.3 jit_solution(18022356369100051946)
XLA Ops:
  0.0 84.1 %shard_map.73 = f32[12,8,96,128]{3,2,1,0:T(8,128)S(1)} custom-call(f32[12,8,96,128]{3,2,1,0:T(8,128)} %pert_hbm.1, bf16[8,8,96,128]{3,2,1,0:T(8,128)(2,1)} %base_hbm.1, bf16[2,32,32]{2,1,0:T(8,128)(2,1)} %sops.1, bf16[2,1024,1024]{2,1,0:T(8,128)(2,1)} %aops.1, bf16[2,384,384]{2,1,0:T(8,128)(2,1)} %nops.1, f32[3,12,12]{2,1,0:T(8,128)} %coup.1, f32[3,12,12]{2,1,0:T(8,128)} %chem.1), custom_call_target="tpu_custom_call" | custom-call | tf_op jit(solution)/shard_map/pallas_call | solution.py:421
  84.1 2.2 %copy.9 = f32[12,8,96,128]{3,2,1,0:T(8,128)} copy(f32[12,8,96,128]{3,2,1,0:T(8,128)S(1)} %shard_map.73) | data formatting | bytes 9437184

commit v4 on v3

--- a/solution.py
+++ b/solution.py
@@ -20,9 +20,13 @@
                 table[name, t, d] = count
                 count += 1
         for d in range(4):
-            for name in ("lo", "hi", "co", "cw"):
+            for name in ("co", "cw"):
                 table[name, t, d] = count
                 count += 1
+            for part in range(2):
+                for name in ("lo", "hi"):
+                    table[name, t, d, part] = count
+                    count += 1
     for g in range(3):
         for d in (1, 2, 3):
             for name in ("yf", "yr"):
@@ -106,14 +110,17 @@
     def src_own(t, d):
         return zs.at[2 * z + t] if d == 0 else gat.at[t, slot_own, z_of(-d)]
 
-    def lo_c(t, d):
-        return remote(src_own(t, d), oth.at[t, z_of(-d)], ("lo", t, d), lo_dev)
+    def piece(ref, part):
+        return ref.at[pl.ds(part * (NV // 2), NV // 2)]
+
+    def lo_c(t, d, part):
+        return remote(piece(src_own(t, d), part), piece(oth.at[t, z_of(-d)], part), ("lo", t, d, part), lo_dev)
 
     def co(t, d):
         return remote(src_own(t, d), gat.at[t, slot_own, z_of(-d)], ("co", t, d), core_dev)
 
-    def hi_c(t, d):
-        return remote(oth.at[t, z_of(-d)], gat.at[t, slot_own, z_of(-d)], ("hi", t, d), hi_dev)
+    def hi_c(t, d, part):
+        return remote(piece(oth.at[t, z_of(-d)], part), piece(gat.at[t, slot_own, z_of(-d)], part), ("hi", t, d, part), hi_dev)
 
     def cw(t, d):
         return remote(gat.at[t, slot_hi, z_of(-d)], gat.at[t, slot_hi, z_of(-d)], ("cw", t, d), core_dev)
@@ -134,13 +141,13 @@
 
     lower(0)
     pl.semaphore_wait(barrier, len(partners))
-    lo_c(0, 0).start()
+    for part in range(2):
+        lo_c(0, 0, part).start()
     co(0, 0).start()
     for i, d in enumerate((1, 3, 2)):
         lower(1 + i)
         zf(0, d).start()
     lower(4)
-    lo_c(1, 0).start()
     co(1, 0).start()
     for i in (5, 6, 7):
         lower(i)
@@ -165,11 +172,10 @@
         for d in (1, 3, 2):
             yf(g, d).start()
     for d in (1, 3, 2):
-        zb(0, d).start()
-    for d in (1, 3, 2):
         zf(1, d).start()
-    for d in (1, 3, 2):
-        zb(1, d).start()
+    for t in range(2):
+        for d in (1, 3, 2):
+            zb(t, d).start()
     yown = []
     for g in range(3):
         yown.append(pltpu.make_async_copy(ys.at[y * 3 + g], yr.at[g, y], lsem.at[8 + g]))
@@ -269,7 +275,7 @@
         for d in (1, 3, 2):
             yret(g, d).start()
 
-    def azimuth(t, own_blocks, other_blocks, fresh):
+    def azimuth(t, own_blocks, other_blocks, fresh, rows=(0, N // 16)):
         def rows_of(q, _):
             r = pl.ds(pl.multiple_of(q * 16, 16), 16)
             x = [gat[t, slot_own, b, :, r, :].reshape(192, A) for b in own_blocks]
@@ -285,7 +291,7 @@
                     da[t, k, b, :, r, :] = part
             return 0
 
-        lax.fori_loop(0, N // 16, rows_of, 0, unroll=2)
+        lax.fori_loop(*rows, rows_of, 0, unroll=3)
 
     def turned_flux(t, d):
         b = z_of(-d)
@@ -322,17 +328,19 @@
         if d:
             zr(t, 4 - d).start()
 
-    def pass_lo(t, d):
-        zf(t, d).wait_recv()
-        lo_c(t, d).start()
-        co(t, d).start()
-
-    def pass_hi(t, d):
-        lo_c(t, d).wait_recv()
-        hi_c(t, d).start()
+    def pass_lo(t, d, part):
+        if d and not part:
+            zf(t, d).wait_recv()
+            co(t, d).start()
+        lo_c(t, d, part).start()
+
+    def pass_hi(t, d, part):
+        lo_c(t, d, part).wait_recv()
+        hi_c(t, d, part).start()
 
     def pass_core(t, d):
-        hi_c(t, d).wait_recv()
+        for part in range(2):
+            hi_c(t, d, part).wait_recv()
         cw(t, d).start()
 
     def add_stream(g, d):
@@ -350,47 +358,65 @@
             src = fz[t, z, v] if d == 0 else rz[st, v]
             out[v, st] += (held if 5 <= v <= 9 else 0.2) * src.astype(F32)
 
-    order = [(0, 0), (1, 0), (0, 1), (0, 3), (0, 2), (1, 1), (1, 3), (1, 2)]
+    order = [(0, 0, 0), (0, 0, 1), (1, 0, 0)]
+    order += [(t, d, part) for t in range(2) for d in ((1, 3, 2)) for part in range(2)] + [(1, 0, 1)]
 
     def step(k):
         pass_hi(*order[k])
-        if k + 2 < 8:
+        if k + 2 < len(order):
             pass_lo(*order[k + 2])
-        if 2 <= k < 7:
-            pass_core(*order[k - 2])
-
-    sources(0, 3)
+
+    first, second = (0, N // 32), (N // 32, N // 16)
+    sources(0, 2)
     step(0)
-    sources(3, 3)
+    sources(2, 1)
     step(1)
+    sources(3, 1)
+    step(2)
+    sources(4, 1)
+    step(3)
+    sources(5, 1)
+    step(4)
+    pass_core(0, 0)
     sources(6, 2)
-    step(2)
+    step(5)
+    step(6)
     stream_flux(0)
-    step(3)
+    step(7)
+    pass_core(0, 1)
     stream_flux(1)
     for w in weights:
         w.wait()
     for c in own:
         c.wait()
-    step(4)
-    azimuth(0, range(4), range(4), True)
-    stream_flux(2)
-    step(5)
+    step(8)
+    azimuth(0, range(4), range(4), True, first)
+    pass_core(0, 3)
+    step(9)
+    azimuth(0, range(4), range(4), True, second)
+    step(10)
     turned_flux(0, 0)
     turned_flux(0, 1)
-    azimuth(1, range(4), [z_of(-d) for d in (0, 1)], True)
-    step(6)
+    pass_core(0, 2)
+    step(11)
     turned_flux(0, 3)
+    stream_flux(2)
+    step(12)
     turned_flux(0, 2)
     pass_core(1, 1)
-    step(7)
-    azimuth(1, [], [z_of(-d) for d in (3, 2)], False)
+    azimuth(1, range(4), [z_of(-d) for d in (1, 3)], True, first)
+    step(13)
+    azimuth(1, range(4), [z_of(-d) for d in (1, 3)], True, second)
+    step(14)
+    pass_core(1, 3)
+    step(15)
+    azimuth(1, [], [z_of(-d) for d in (2, 0)], False)
     turned_flux(1, 1)
-    pass_core(1, 3)
     turned_flux(1, 3)
-    turned_flux(1, 0)
     pass_core(1, 2)
     turned_flux(1, 2)
+    pass_core(1, 0)
+    turned_flux(1, 0)
     for g in range(3):
         add_stream(g, 0)
         for d in (1, 3, 2):
@@ -403,8 +429,11 @@
             add_turned(t, d)
     for t in range(2):
         for d in range(4):
-            for copy in (lo_c, co, hi_c, cw):
+            for copy in (co, cw):
                 copy(t, d).wait_send()
+            for part in range(2):
+                lo_c(t, d, part).wait_send()
+                hi_c(t, d, part).wait_send()
         for d in (1, 2, 3):
             for copy in (zf, zb, zr):
                 copy(t, d).wait_send()

time: 86.4 us -> 82.8 us (0.958)
  Pallas kernels: 84.1 us -> 80.5 us
    pallas_call x1, Pallas kernels: 84.1 us -> 80.5 us  [shards(): pl.pallas_call(kernel, out_shape=pltpu.VMEM(perturbation.shape, F32), in_...]
where the time goes in v4:
time: 82.8 us; the launch traced here: 82.7 us
  Pallas kernels  80.5 us (97%)
  local copies, waits for them, and re-layouts  2.19 us (3%)
    pallas_call x1, Pallas kernels, shards(): pl.pallas_call(kernel, out_shape=pltpu.VMEM(perturbation.shape, F32), in_...  80.5 us
    unnamed x1, local copies, waits for them, and re-layouts  2.19 us

profile of v4, /device:TPU:1, one launch (start us, length us, event | category | flops | bytes accessed | tf_op | source)
XLA Modules:
  0.0 82.7 jit_solution(6821471152574127924)
XLA Ops:
  0.0 80.5 %shard_map.73 = f32[12,8,96,128]{3,2,1,0:T(8,128)S(1)} custom-call(f32[12,8,96,128]{3,2,1,0:T(8,128)} %pert_hbm.1, bf16[8,8,96,128]{3,2,1,0:T(8,128)(2,1)} %base_hbm.1, bf16[2,32,32]{2,1,0:T(8,128)(2,1)} %sops.1, bf16[2,1024,1024]{2,1,0:T(8,128)(2,1)} %aops.1, bf16[2,384,384]{2,1,0:T(8,128)(2,1)} %nops.1, f32[3,12,12]{2,1,0:T(8,128)} %coup.1, f32[3,12,12]{2,1,0:T(8,128)} %chem.1), custom_call_target="tpu_custom_call" | custom-call | tf_op jit(solution)/shard_map/pallas_call | solution.py:450
  80.5 2.2 %copy.9 = f32[12,8,96,128]{3,2,1,0:T(8,128)} copy(f32[12,8,96,128]{3,2,1,0:T(8,128)S(1)} %shard_map.73) | data formatting | bytes 9437184

commit v5 on v4

--- a/solution.py
+++ b/solution.py
@@ -10,6 +10,9 @@
 MESH = pl.DeviceIdType.MESH
 F32, BF16 = jnp.float32, jnp.bfloat16
 NV, S, N, A = 12, 8, 96, 128
+
+
+PARTS = 4
 
 
 def copies_table():
@@ -20,10 +23,12 @@
                 table[name, t, d] = count
                 count += 1
         for d in range(4):
-            for name in ("co", "cw"):
-                table[name, t, d] = count
+            table["co", t, d] = count
+            count += 1
+            for part in range(2):
+                table["cw", t, d, part] = count
                 count += 1
-            for part in range(2):
+            for part in range(PARTS):
                 for name in ("lo", "hi"):
                     table[name, t, d, part] = count
                     count += 1
@@ -57,8 +62,8 @@
     return high, (matrix - high.astype(F32)).astype(BF16)
 
 
-def kernel(pert_hbm, base_hbm, sops, aops, nops, coup, chem, out,
-           pert, base, zs, zbs, gat, zbase, oth, ys, yr, fy, ry, fz, rz, da, dn, dy, wa, kc, ky, kz, ks, kn,
+def kernel(pert_hbm, base_hbm, sops_hbm, aops, nops_hbm, coup_hbm, chem_hbm, out,
+           pert, base, sops, nops, coup, chem, zs, zbs, gat, zbase, oth, ys, yr, fy, ry, fz, rz, da, dn, dy, wa, kc, ky, kz, ks, kn,
            ssem, rsem, lsem, isem, wsem):
     y = lax.axis_index("stream")
     ai = lax.axis_index("azim")
@@ -88,6 +93,10 @@
     for pair in loads:
         for load in pair:
             load.start()
+    small = [pltpu.make_async_copy(far, near, isem.at[2 * S + i]) for i, (far, near) in enumerate(
+        ((sops_hbm, sops), (nops_hbm, nops), (coup_hbm, coup), (chem_hbm, chem)))]
+    for load in small:
+        load.start()
     barrier = pltpu.get_barrier_semaphore()
     partners = [at(y_=y_of(d)) for d in (1, 2, 3)] + [at(z_=z_of(d)) for d in (1, 2, 3)] + [lo_dev, hi_dev, core_dev]
     for device in partners:
@@ -110,8 +119,8 @@
     def src_own(t, d):
         return zs.at[2 * z + t] if d == 0 else gat.at[t, slot_own, z_of(-d)]
 
-    def piece(ref, part):
-        return ref.at[pl.ds(part * (NV // 2), NV // 2)]
+    def piece(ref, part, parts=PARTS):
+        return ref.at[pl.ds(part * (NV // parts), NV // parts)]
 
     def lo_c(t, d, part):
         return remote(piece(src_own(t, d), part), piece(oth.at[t, z_of(-d)], part), ("lo", t, d, part), lo_dev)
@@ -122,8 +131,9 @@
     def hi_c(t, d, part):
         return remote(piece(oth.at[t, z_of(-d)], part), piece(gat.at[t, slot_own, z_of(-d)], part), ("hi", t, d, part), hi_dev)
 
-    def cw(t, d):
-        return remote(gat.at[t, slot_hi, z_of(-d)], gat.at[t, slot_hi, z_of(-d)], ("cw", t, d), core_dev)
+    def cw(t, d, part):
+        here = piece(gat.at[t, slot_hi, z_of(-d)], part, 2)
+        return remote(here, here, ("cw", t, d, part), core_dev)
 
     def yf(g, d):
         return remote(ys.at[y_of(d) * 3 + g], yr.at[g, y], ("yf", g, d), at(y_=y_of(d)))
@@ -141,7 +151,7 @@
 
     lower(0)
     pl.semaphore_wait(barrier, len(partners))
-    for part in range(2):
+    for part in range(PARTS):
         lo_c(0, 0, part).start()
     co(0, 0).start()
     for i, d in enumerate((1, 3, 2)):
@@ -190,6 +200,8 @@
     for w in weights:
         w.start()
 
+    for load in small:
+        load.wait()
     ks[...] = spread(sops[...].reshape(64, 32), 8)
     c_high, c_low = split_two(coup[...])
     ky[:, 0:192] = spread(c_high[0], 16)
@@ -296,7 +308,8 @@
     def turned_flux(t, d):
         b = z_of(-d)
         co(t, d).wait_recv()
-        cw(t, d).wait_recv()
+        for part in range(2):
+            cw(t, d, part).wait_recv()
         if d:
             zb(t, d).wait_recv()
 
@@ -340,8 +353,9 @@
 
     def pass_core(t, d):
         for part in range(2):
-            hi_c(t, d, part).wait_recv()
-        cw(t, d).start()
+            for quarter in (2 * part, 2 * part + 1):
+                hi_c(t, d, quarter).wait_recv()
+            cw(t, d, part).start()
 
     def add_stream(g, d):
         i = y_of(-d) * 3 + g
@@ -358,13 +372,15 @@
             src = fz[t, z, v] if d == 0 else rz[st, v]
             out[v, st] += (held if 5 <= v <= 9 else 0.2) * src.astype(F32)
 
-    order = [(0, 0, 0), (0, 0, 1), (1, 0, 0)]
-    order += [(t, d, part) for t in range(2) for d in ((1, 3, 2)) for part in range(2)] + [(1, 0, 1)]
-
-    def step(k):
-        pass_hi(*order[k])
-        if k + 2 < len(order):
-            pass_lo(*order[k + 2])
+    order = [(0, 0, part) for part in range(4)] + [(1, 0, part) for part in [0]]
+    order += [(t, d, part) for t in range(2) for d in (1, 3, 2) for part in range(4)]
+    order += [(1, 0, part) for part in [1, 2, 3]]
+
+    def step(half):
+        for k in (2 * half, 2 * half + 1):
+            pass_hi(*order[k])
+            if k + 4 < len(order):
+                pass_lo(*order[k + 4])
 
     first, second = (0, N // 32), (N // 32, N // 16)
     sources(0, 2)
@@ -429,9 +445,10 @@
             add_turned(t, d)
     for t in range(2):
         for d in range(4):
-            for copy in (co, cw):
-                copy(t, d).wait_send()
+            co(t, d).wait_send()
             for part in range(2):
+                cw(t, d, part).wait_send()
+            for part in range(PARTS):
                 lo_c(t, d, part).wait_send()
                 hi_c(t, d, part).wait_send()
         for d in (1, 2, 3):
@@ -450,11 +467,15 @@
     return pl.pallas_call(
         kernel,
         out_shape=pltpu.VMEM(perturbation.shape, F32),
-        in_specs=[hbm, hbm, vmem, hbm, vmem, vmem, vmem],
+        in_specs=[hbm] * 7,
         out_specs=vmem,
         scratch_shapes=[
             pltpu.VMEM((NV, S, N, A), F32),
             scratch(8, S, N, A),
+            scratch(2, 32, 32),
+            scratch(2, 384, 384),
+            pltpu.VMEM((3, NV, NV), F32),
+            pltpu.VMEM((3, NV, NV), F32),
             scratch(S, NV, N, A),
             scratch(S, 4, N, A),
             scratch(2, 4, 4, NV, N, A),
@@ -478,7 +499,7 @@
             pltpu.SemaphoreType.DMA((COPIES,)),
             pltpu.SemaphoreType.DMA((COPIES,)),
             pltpu.SemaphoreType.DMA((11,)),
-            pltpu.SemaphoreType.DMA((2 * S,)),
+            pltpu.SemaphoreType.DMA((2 * S + 4,)),
             pltpu.SemaphoreType.DMA((16,)),
         ],
         compiler_params=pltpu.CompilerParams(collective_id=0, has_side_effects=True, vmem_limit_bytes=56 << 20),

time: 82.8 us -> 81.5 us (0.984); the launches traced: 82.7 us -> 80.5 us
  Pallas kernels: 80.5 us -> 78.3 us
    pallas_call x1, Pallas kernels: 80.5 us -> 78.3 us  [shards(): pl.pallas_call(kernel, out_shape=pltpu.VMEM(perturbation.shape, F32), in_...]
where the time goes in v5:
time: 81.5 us; the launch traced here: 80.5 us
  Pallas kernels  78.3 us (96%)
  local copies, waits for them, and re-layouts  2.19 us (3%)
    pallas_call x1, Pallas kernels, shards(): pl.pallas_call(kernel, out_shape=pltpu.VMEM(perturbation.shape, F32), in_...  78.3 us
    unnamed x1, local copies, waits for them, and re-layouts  2.19 us

profile of v5, /device:TPU:1, one launch (start us, length us, event | category | flops | bytes accessed | tf_op | source)
XLA Modules:
  0.0 80.5 jit_solution(9413559147949743546)
XLA Ops:
  0.0 78.3 %shard_map.73 = f32[12,8,96,128]{3,2,1,0:T(8,128)S(1)} custom-call(f32[12,8,96,128]{3,2,1,0:T(8,128)} %pert_hbm.1, bf16[8,8,96,128]{3,2,1,0:T(8,128)(2,1)} %base_hbm.1, bf16[2,32,32]{2,1,0:T(8,128)(2,1)} %sops_hbm.1, bf16[2,1024,1024]{2,1,0:T(8,128)(2,1)} %aops.1, bf16[2,384,384]{2,1,0:T(8,128)(2,1)} %nops_hbm.1, f32[3,12,12]{2,1,0:T(8,128)} %coup_hbm.1, ...), custom_call_target="tpu_custom_call" | custom-call | tf_op jit(solution)/shard_map/pallas_call | solution.py:467
  78.3 2.2 %copy.9 = f32[12,8,96,128]{3,2,1,0:T(8,128)} copy(f32[12,8,96,128]{3,2,1,0:T(8,128)S(1)} %shard_map.73) | data formatting | bytes 9437184

commit v6 on v5

--- a/solution.py
+++ b/solution.py
@@ -425,8 +425,9 @@
     azimuth(1, range(4), [z_of(-d) for d in (1, 3)], True, second)
     step(14)
     pass_core(1, 3)
+    azimuth(1, [], [z_of(-2)], False)
     step(15)
-    azimuth(1, [], [z_of(-d) for d in (2, 0)], False)
+    azimuth(1, [], [z], False)
     turned_flux(1, 1)
     turned_flux(1, 3)
     pass_core(1, 2)

time: 81.5 us -> 81.1 us (level)
  no operation moved by 1% of the time
where the time goes in v6:
time: 81.1 us; the launch traced here: 80.3 us
  Pallas kernels  78.1 us (96%)
  local copies, waits for them, and re-layouts  2.19 us (3%)
    pallas_call x1, Pallas kernels, shards(): pl.pallas_call(kernel, out_shape=pltpu.VMEM(perturbation.shape, F32), in_...  78.1 us
    unnamed x1, local copies, waits for them, and re-layouts  2.19 us

profile of v6, /device:TPU:1, one launch (start us, length us, event | category | flops | bytes accessed | tf_op | source)
XLA Modules:
  0.0 80.3 jit_solution(1015697880082806018)
XLA Ops:
  0.0 78.1 %shard_map.73 = f32[12,8,96,128]{3,2,1,0:T(8,128)S(1)} custom-call(f32[12,8,96,128]{3,2,1,0:T(8,128)} %pert_hbm.1, bf16[8,8,96,128]{3,2,1,0:T(8,128)(2,1)} %base_hbm.1, bf16[2,32,32]{2,1,0:T(8,128)(2,1)} %sops_hbm.1, bf16[2,1024,1024]{2,1,0:T(8,128)(2,1)} %aops.1, bf16[2,384,384]{2,1,0:T(8,128)(2,1)} %nops_hbm.1, f32[3,12,12]{2,1,0:T(8,128)} %coup_hbm.1, ...), custom_call_target="tpu_custom_call" | custom-call | tf_op jit(solution)/shard_map/pallas_call | solution.py:468
  78.1 2.2 %copy.9 = f32[12,8,96,128]{3,2,1,0:T(8,128)} copy(f32[12,8,96,128]{3,2,1,0:T(8,128)S(1)} %shard_map.73) | data formatting | bytes 9437184
